TPU v7x, 32 devices: a whole 2x2x4 slice. The times are simulated.
32 devices in a mesh: tm: 4 (over x, core), space: 8 (over z, y).
Axes of the slice: x: 2, y: 2, z: 4, core: 2. Of those that a mesh axis runs over, the one named last changes fastest.
Arguments:
- field: float32 [2048, 128, 256], P('tm', 'space'), may hold values from -6 to 6
- mask: int32 [2048, 128, 256], P('tm', 'space'), may hold values 0 or 1
- noise: float32 [128, 256], P('space'), may hold values from 0.1 to 1
- lat_factor: float32 [128, 128], replicated, may hold values from -1 to 2.5, as said below
- lon_factor: float32 [256, 256], replicated, may hold values from -1 to 2.5, as said below
- time_tiles: float32 [5, 128, 128], replicated, may hold values from -1 to 2.5, as said below
- amplitude: float32 [16], replicated, may hold values from 0.5 to 2
- depth: int32 [16], replicated, may hold values from 0 to 4
Outputs:
- product: float32 [2048, 128, 256], P('tm', 'space')
Inputs may be any that keep to these rules, and one draw needn't show every extreme that they name: `lat_factor`: symmetric. `lon_factor`: symmetric. time_tiles[0] is symmetric.
All inputs are finite; a program needn't handle non-finite values. No bound on the sum of `mask` on one device may be relied on, other than what follows from the above.
Results may differ from a plain program's by a relative error of at most 0.0001.
Values sent between devices are 32-bit elements; how exact they have to be, the bound alone decides.
No kernel may reach another device: no remote copies, remote signals or barrier semaphores. Data moves between devices by JAX's collectives and lax.ppermute only.
A program may use at most 192 MiB of HBM per device.

v0:
```python
import jax
import jax.numpy as jnp
from jax import lax
from jax.sharding import PartitionSpec as P

HB = 128


def from_behind(value, axis, steps):
    count = lax.axis_size(axis)
    initial, last = (max(0, -steps), min(count, count - steps))
    return lax.ppermute(value, axis, [(source, source + steps) for source in range(initial, last)])


def band(padded, depth_pad, first_block, block_count, time_tiles):
    highest = lax.Precision.HIGHEST
    result = jnp.einsum(
        "ij,bjs->bis", time_tiles[0], padded[4 : 4 + block_count], precision=highest
    )
    for offset in range(1, 5):
        depth_here = lax.dynamic_slice_in_dim(depth_pad, first_block + 4, block_count)
        depth_before = lax.dynamic_slice_in_dim(depth_pad, first_block + 4 - offset, block_count)
        weight_above = (depth_here >= offset).astype(jnp.float32)
        weight_below = (depth_before >= offset).astype(jnp.float32)
        above_data = padded[4 + offset : 4 + offset + block_count]
        below_data = padded[4 - offset : 4 - offset + block_count]
        tile = time_tiles[offset]

        def above_product(tile=tile, above_data=above_data, weight_above=weight_above):
            return weight_above[:, None, None] * jnp.einsum(
                "ij,bjs->bis", tile, above_data, precision=highest
            )

        def below_product(tile=tile, below_data=below_data, weight_below=weight_below):
            return weight_below[:, None, None] * jnp.einsum(
                "ji,bjs->bis", tile, below_data, precision=highest
            )

        above_term = above_product()
        below_term = below_product()
        result = result + above_term + below_term
    return result


def per_device(field, mask, noise, lat_factor, lon_factor, time_tiles, amplitude, depth):
    highest = lax.Precision.HIGHEST
    hour_count = field.shape[0]
    local_blocks = hour_count // HB
    masked = mask.astype(jnp.float32) * field
    depth_pad = jnp.pad(depth, 4)
    rows_done = jnp.einsum("him,lm->hil", masked, lon_factor, precision=highest)
    columns = jnp.einsum(
        "ij,hjl->hil",
        lat_factor,
        lax.all_to_all(rows_done, "space", split_axis=2, concat_axis=1, tiled=True),
        precision=highest,
    )
    cell_count = columns.shape[1] * columns.shape[2]
    start_block = lax.axis_index("tm") * local_blocks
    local_amp = lax.dynamic_slice_in_dim(amplitude, start_block, local_blocks)
    scaled = columns.reshape(local_blocks, HB, cell_count) * local_amp[:, None, None]
    below_parts = from_behind(scaled, "tm", 1)
    above_parts = from_behind(scaled, "tm", -1)
    padded = jnp.concatenate([below_parts, scaled, above_parts], axis=0)
    banded = (
        band(padded, depth_pad, start_block, local_blocks, time_tiles) * local_amp[:, None, None]
    )
    banded = banded.reshape(hour_count, columns.shape[1], columns.shape[2])
    result = lax.all_to_all(banded, "space", split_axis=1, concat_axis=2, tiled=True)
    return mask.astype(jnp.float32) * result + noise[None] * field


def solution(mesh):
    in_specs = (
        P("tm", "space", None),
        P("tm", "space", None),
        P("space", None),
        P(),
        P(),
        P(),
        P(),
        P(),
    )
    out_specs = P("tm", "space", None)
    return jax.shard_map(
        per_device, mesh=mesh, in_specs=in_specs, out_specs=out_specs, check_vma=False
    )
```

profile of v0, /device:TPU:10, one launch (start us, length us, event | category | flops | bytes accessed | tf_op | source)
XLA Modules:
  0.0 676.2 jit_solution(15521888110722495024)
XLA Ops:
  0.0 0.0 copy-start
  0.0 9.9 %copy.26 = f32[512,16,256]{0,2,1:T(8,128)} copy(f32[512,16,256]{2,1,0:T(8,128)} %param.8) | data formatting | bytes 16777216 | tf_op args[0]
  10.0 10.0 %copy.25 = s32[512,16,256]{0,2,1:T(8,128)} copy(s32[512,16,256]{2,1,0:T(8,128)} %param.9) | data formatting | bytes 16777216 | tf_op args[1]
  20.0 0.0 copy-done
  20.0 18.8 %fusion.11 = f32[512,16,256]{2,0,1:T(8,128)} fusion(f32[512,16,256]{0,2,1:T(8,128)} %copy.26, s32[512,16,256]{0,2,1:T(8,128)} %copy.25, f32[256,256]{1,0:T(8,128)S(1)} %copy-done), kind=kOutput, calls=%fused_computation.16 | convolution fusion | flops 6446645248 | bytes 25427968 | tf_op jit(solution)/shard_map/him,lm->hil/dot_general | solution.py:51
  38.8 10.4 %copy.28 = f32[512,16,256]{0,1,2:T(8,128)} copy(f32[512,16,256]{2,0,1:T(8,128)} %fusion.11) | data formatting | bytes 16777216 | tf_op jit(solution)/shard_map/him,lm->hil/dot_general | solution.py:51
  49.3 0.0 copy-start.6
  49.3 6.9 %all-to-all-start = ((f32[512,16,256]{0,1,2:T(8,128)}), f32[512,16,256]{0,1,2:T(8,128)}, u32[]{:S(2)}, u32[]{:S(2)}) async-start(f32[512,16,256]{0,1,2:T(8,128)} %copy.28), calls=%async_computation | async-start | bytes 16777216 | tf_op jit(solution)/shard_map/all_to_all | solution.py:55
  56.2 0.0 copy-done.6
  56.2 0.1 dynamic_slice.21
  56.3 0.1 broadcast_bitcast_fusion
  56.4 180.4 %all-to-all-done = f32[512,16,256]{0,1,2:T(8,128)} async-done(((f32[512,16,256]{0,1,2:T(8,128)}), f32[512,16,256]{0,1,2:T(8,128)}, u32[]{:S(2)}, u32[]{:S(2)}) %all-to-all-start) | async-done | bytes 8388640 | tf_op jit(solution)/shard_map/all_to_all | solution.py:55
  236.7 0.0 copy-start.3
  236.7 8.1 %copy.30 = f32[512,8,16,32]{0,3,2,1:T(8,128)S(1)} copy(f32[512,8,16,32]{0,2,3,1:T(8,128)} %bitcast.3) | data formatting | bytes 16777216 | tf_op jit(solution)/shard_map/all_to_all | solution.py:55
  244.9 0.0 copy-done.3
  244.9 19.1 %broadcast_multiply_fusion = (f32[512,128,32]{1,0,2:T(8,128)}, f32[512,128,32]{1,0,2:T(8,128)}) fusion(f32[512]{0:T(512)S(1)} %broadcast_bitcast_fusion, f32[128,128]{1,0:T(8,128)S(1)} %copy-done.3, f32[512,128,32]{0,2,1:T(8,128)S(1)} %bitcast.65), kind=kOutput, calls=%fused_computation.19 | convolution fusion | flops 3223322624 | bytes 25233408 | tf_op jit(solution)/shard_map/ij,hjl->hil/dot_general | solution.py:52
  264.0 10.3 %copy.34 = f32[512,128,32]{0,2,1:T(8,128)} copy(f32[512,128,32]{1,0,2:T(8,128)} %get-tuple-element.17) | data formatting | bytes 16777216 | tf_op jit(solution)/shard_map/ij,hjl->hil/transpose | solution.py:52
  274.3 9.9 %reshape.18 = f32[4,128,4096]{1,0,2:T(4,128)} reshape(f32[512,128,32]{0,2,1:T(8,128)} %copy.34) | data formatting | bytes 16777216 | tf_op jit(solution)/shard_map/reshape | solution.py:61
  284.2 0.0 copy-start.5
  284.2 7.2 %copy_multiply_fusion = f32[4,128,4096]{1,2,0:T(8,128)} fusion(f32[4,128,4096]{1,0,2:T(4,128)} %reshape.18, f32[4]{0:T(128)S(1)} %dynamic_slice.21), kind=kLoop, calls=%fused_computation.10 | loop fusion | flops 2097152 | bytes 16777232 | tf_op jit(solution)/shard_map/mul | solution.py:61
  291.4 1.9 collective-permute-start.1
  293.4 3.8 collective-permute-start
  297.2 0.0 copy-done.5
  297.2 0.1 compare_convert_fusion.6
  297.3 10.4 %copy.32 = f32[512,128,32]{0,2,1:T(8,128)} copy(f32[512,128,32]{1,0,2:T(8,128)} %get-tuple-element.16) | data formatting | bytes 16777216 | tf_op jit(solution)/shard_map/mul | solution.py:61
  307.7 0.0 copy-start.2
  307.7 10.0 %mul.130 = f32[4,128,4096]{1,0,2:T(4,128)} reshape(f32[512,128,32]{0,2,1:T(8,128)} %copy.32) | data formatting | bytes 16777216 | tf_op jit(solution)/shard_map/mul | solution.py:61
  317.7 0.0 copy-done.2
  317.7 11.1 %fusion.7 = f32[4,4096,128]{2,1,0:T(8,128)} fusion(f32[4,128,4096]{1,0,2:T(4,128)} %mul.130, f32[5,128,128]{2,1,0:T(8,128)S(1)} %copy-done.2), kind=kOutput, calls=%fused_computation.11 | convolution fusion | flops 3221225472 | bytes 16842752 | tf_op jit(solution)/shard_map/ij,bjs->bis/dot_general | solution.py:17
  328.8 57.7 %collective-permute-done.1 = f32[4,128,4096]{1,2,0:T(8,128)} collective-permute-done((f32[4,128,4096]{1,2,0:T(8,128)}, f32[4,128,4096]{1,2,0:T(8,128)}, u32[]{:S(2)}, u32[]{:S(2)}) %collective-permute-start.1) | collective-permute-done | bytes 8388640 | tf_op jit(solution)/shard_map/ppermute | solution.py:12
  386.5 10.7 %fusion.1 = f32[4,4096,128]{2,1,0:T(8,128)} fusion(f32[4,128,4096]{1,2,0:T(8,128)} %copy_multiply_fusion, f32[4,128,4096]{1,2,0:T(8,128)} %collective-permute-done.1, f32[5,128,128]{2,1,0:T(8,128)S(1)} %copy-done.2), kind=kOutput, calls=%fused_computation.3 | convolution fusion | flops 3225419776 | bytes 25231360 | tf_op jit(solution)/shard_map/ji,bjs->bis/dot_general | solution.py:35
  397.3 10.8 %fusion = f32[4,4096,128]{2,1,0:T(8,128)} fusion(f32[4,128,4096]{1,2,0:T(8,128)} %copy_multiply_fusion, f32[4,128,4096]{1,2,0:T(8,128)} %collective-permute-done.1, f32[5,128,128]{2,1,0:T(8,128)S(1)} %copy-done.2), kind=kOutput, calls=%fused_computation.2 | convolution fusion | flops 3225419776 | bytes 25231360 | tf_op jit(solution)/shard_map/ji,bjs->bis/dot_general | solution.py:35
  408.1 10.7 %fusion.2 = f32[4,4096,128]{2,1,0:T(8,128)} fusion(f32[4,128,4096]{1,2,0:T(8,128)} %copy_multiply_fusion, f32[4,128,4096]{1,2,0:T(8,128)} %collective-permute-done.1, f32[5,128,128]{2,1,0:T(8,128)S(1)} %copy-done.2), kind=kOutput, calls=%fused_computation.4 | convolution fusion | flops 3225419776 | bytes 25231360 | tf_op jit(solution)/shard_map/ji,bjs->bis/dot_general | solution.py:35
  418.8 0.0 collective-permute-done
  418.8 11.0 %fusion.4 = f32[4,4096,128]{2,1,0:T(8,128)} fusion(f32[4,128,4096]{1,2,0:T(8,128)} %collective-permute-done, f32[4,128,4096]{1,2,0:T(8,128)} %copy_multiply_fusion, f32[5,128,128]{2,1,0:T(8,128)S(1)} %copy-done.2), kind=kOutput, calls=%fused_computation.6 | convolution fusion | flops 3225419776 | bytes 25231360 | tf_op jit(solution)/shard_map/ij,bjs->bis/dot_general | solution.py:30
  429.8 10.7 %fusion.3 = f32[4,4096,128]{2,1,0:T(8,128)} fusion(f32[4,128,4096]{1,2,0:T(8,128)} %collective-permute-done, f32[4,128,4096]{1,2,0:T(8,128)} %copy_multiply_fusion, f32[5,128,128]{2,1,0:T(8,128)S(1)} %copy-done.2), kind=kOutput, calls=%fused_computation.5 | convolution fusion | flops 3225419776 | bytes 25231360 | tf_op jit(solution)/shard_map/ij,bjs->bis/dot_general | solution.py:30
  440.6 10.9 %fusion.5 = f32[4,4096,128]{2,1,0:T(8,128)} fusion(f32[4,128,4096]{1,2,0:T(8,128)} %collective-permute-done, f32[4,128,4096]{1,2,0:T(8,128)} %copy_multiply_fusion, f32[5,128,128]{2,1,0:T(8,128)S(1)} %copy-done.2), kind=kOutput, calls=%fused_computation.7 | convolution fusion | flops 3225419776 | bytes 25231360 | tf_op jit(solution)/shard_map/ij,bjs->bis/dot_general | solution.py:30
  451.5 10.9 %fusion.19 = f32[4,4096,128]{2,1,0:T(8,128)} fusion(f32[4,128,4096]{1,2,0:T(8,128)} %collective-permute-done, f32[5,128,128]{2,1,0:T(8,128)S(1)} %copy-done.2), kind=kOutput, calls=%fused_computation.23 | convolution fusion | flops 3221225472 | bytes 16842752 | tf_op jit(solution)/shard_map/ij,bjs->bis/dot_general | solution.py:30
  462.4 30.0 %multiply_bitcast_fusion = f32[4,128,4096]{1,2,0:T(8,128)} fusion(f32[4,4096,128]{2,1,0:T(8,128)} %fusion.19, f32[4,4096,128]{2,1,0:T(8,128)} %fusion, f32[4,4096,128]{2,1,0:T(8,128)} %fusion.3, f32[4,4096,128]{2,1,0:T(8,128)} %fusion.1, f32[4,4096,128]{2,1,0:T(8,128)} %fusion.4, f32[4,4096,128]{2,1,0:T(8,128)} %fusion.2, f32[4,4096,128]{2,1,0:T(8,128)} %fusion.7, ...), kind=kOutput, calls=%fused_computation.15 | convolution fusion | flops 3256877056 | bytes 83956224 | tf_op jit(solution)/shard_map/ji,bjs->bis/dot_general | solution.py:35
  492.4 11.8 %copy.36 = f32[4,128,4096]{1,0,2:T(4,128)} copy(f32[4,128,4096]{1,2,0:T(8,128)} %multiply_bitcast_fusion) | data formatting | bytes 16777216 | tf_op jit(solution)/shard_map/mul | solution.py:66
  504.2 10.3 %reshape.19 = f32[512,128,32]{0,2,1:T(8,128)} reshape(f32[4,128,4096]{1,0,2:T(4,128)} %copy.36) | data formatting | bytes 16777216 | tf_op jit(solution)/shard_map/reshape | solution.py:68
  514.5 0.0 slice-start
  514.5 0.0 slice-start.2
  514.5 136.0 %all_to_all.36 = f32[512,128,32]{0,2,1:T(8,128)} all-to-all(f32[512,128,32]{0,2,1:T(8,128)} %reshape.19), channel_id=1, replica_groups=mesh['tm'=4,'space'=8] {'space'}, dimensions={1} | all-to-all | bytes 16777216 | tf_op jit(solution)/shard_map/all_to_all | solution.py:69
  650.6 0.0 slice-start.1
  650.6 0.0 slice-start.3
  650.6 0.0 copy-start.4
  650.6 8.6 %copy.37 = f32[512,16,8,32]{0,3,2,1:T(8,128)} copy(f32[512,16,8,32]{0,3,1,2:T(8,128)} %bitcast.66) | data formatting | bytes 16777216 | tf_op jit(solution)/shard_map/all_to_all | solution.py:69
  659.2 0.0 slice-done
  659.2 0.0 slice-done.2
  659.2 0.0 slice-done.1
  659.2 0.0 slice-done.3
  659.2 0.0 copy-done.4
  659.2 0.0 copy-start.1
  659.2 6.3 fusion.6
  665.5 10.2 %copy.39 = f32[512,16,256]{2,1,0:T(8,128)} copy(f32[512,16,256]{0,2,1:T(8,128)} %fusion.6) | data formatting | bytes 16777216 | tf_op jit(solution)/shard_map/add | solution.py:70
  675.8 0.0 copy-done.1
  (3 shorter events, 0.0 us)
Async XLA Ops:
  0.0 20.0 %copy-start = (f32[256,256]{1,0:T(8,128)S(1)}, f32[256,256]{1,0:T(8,128)}, u32[]{:S(2)}) copy-start(f32[256,256]{1,0:T(8,128)} %param.12) | copy-start | bytes 786436
  49.3 6.9 %copy-start.6 = (f32[16]{0:T(128)S(1)}, f32[16]{0:T(128)}, u32[]{:S(2)}) copy-start(f32[16]{0:T(128)} %param.14) | copy-start | bytes 196
  49.3 187.5 %all-to-all-start = ((f32[512,16,256]{0,1,2:T(8,128)}), f32[512,16,256]{0,1,2:T(8,128)}, u32[]{:S(2)}, u32[]{:S(2)}) async-start(f32[512,16,256]{0,1,2:T(8,128)} %copy.28), calls=%async_computation | async-start | bytes 16777216 | tf_op jit(solution)/shard_map/all_to_all | solution.py:55
  236.7 8.2 %copy-start.3 = (f32[128,128]{1,0:T(8,128)S(1)}, f32[128,128]{1,0:T(8,128)}, u32[]{:S(2)}) copy-start(f32[128,128]{1,0:T(8,128)} %param.11) | copy-start | bytes 196612
  284.2 13.0 %copy-start.5 = (s32[16]{0:T(128)S(1)}, s32[16]{0:T(128)}, u32[]{:S(2)}) copy-start(s32[16]{0:T(128)} %param.15) | copy-start | bytes 196
  291.4 95.1 %collective-permute-start.1 = (f32[4,128,4096]{1,2,0:T(8,128)}, f32[4,128,4096]{1,2,0:T(8,128)}, u32[]{:S(2)}, u32[]{:S(2)}) collective-permute-start(f32[4,128,4096]{1,2,0:T(8,128)} %copy_multiply_fusion), channel_id=1, source_target_pairs={{0,8},{8,16},{16,24},{1,9},{9,17},{17,25},{2,10},{10,18},{18,26},{... | collective-permute-start | bytes 25165832 | tf_op jit(solution)/shard_map/ppermute | solution.py:12
  293.4 125.4 %collective-permute-start = (f32[4,128,4096]{1,2,0:T(8,128)}, f32[4,128,4096]{1,2,0:T(8,128)}, u32[]{:S(2)}, u32[]{:S(2)}) collective-permute-start(f32[4,128,4096]{1,2,0:T(8,128)} %copy_multiply_fusion), channel_id=1, source_target_pairs={{8,0},{16,8},{24,16},{9,1},{17,9},{25,17},{10,2},{18,10},{26,18},{... | collective-permute-start | bytes 25165832 | tf_op jit(solution)/shard_map/ppermute | solution.py:12
  307.7 10.0 %copy-start.2 = (f32[5,128,128]{2,1,0:T(8,128)S(1)}, f32[5,128,128]{2,1,0:T(8,128)}, u32[]{:S(2)}) copy-start(f32[5,128,128]{2,1,0:T(8,128)} %param.13) | copy-start | bytes 983044
  514.5 144.7 %slice-start = ((s8[8388608]{0:T(1024)(128)(4,1)}), s8[4194304]{0:T(1024)(128)(4,1)S(1)}, s32[]{:S(2)}) async-start(s8[8388608]{0:T(1024)(128)(4,1)} %bitcast.61), calls=%async_computation.2 | async-start | bytes 8388608
  514.5 144.7 %slice-start.2 = ((s8[8388608]{0:T(1024)(128)(4,1)}), s8[4194304]{0:T(1024)(128)(4,1)S(1)}, s32[]{:S(2)}) async-start(s8[8388608]{0:T(1024)(128)(4,1)} %bitcast.63), calls=%async_computation.4 | async-start | bytes 8388608
  650.6 8.6 %slice-start.1 = ((s8[8388608]{0:T(1024)(128)(4,1)}), s8[4194304]{0:T(1024)(128)(4,1)S(1)}, s32[]{:S(2)}) async-start(s8[8388608]{0:T(1024)(128)(4,1)} %bitcast.61), calls=%async_computation.3 | async-start | bytes 8388608
  650.6 8.6 %slice-start.3 = ((s8[8388608]{0:T(1024)(128)(4,1)}), s8[4194304]{0:T(1024)(128)(4,1)S(1)}, s32[]{:S(2)}) async-start(s8[8388608]{0:T(1024)(128)(4,1)} %bitcast.63), calls=%async_computation.5 | async-start | bytes 8388608
  650.6 8.6 %copy-start.4 = (f32[16,256]{1,0:T(8,128)S(1)}, f32[16,256]{1,0:T(8,128)}, u32[]{:S(2)}) copy-start(f32[16,256]{1,0:T(8,128)} %param.10) | copy-start | bytes 49156
  659.2 16.5 %copy-start.1 = (f32[256,256]{1,0:T(8,128)S(1)}, f32[256,256]{1,0:T(8,128)}, u32[]{:S(2)}) copy-start(f32[256,256]{1,0:T(8,128)} %param.12) | copy-start | bytes 786436
where the time goes:
time: 685 us; the launch traced here: 676 us
  waiting for transfers between devices  238 us (35%)
  matrix products  155 us (23%)
  blocking collectives  136 us (20%)
  local copies, waits for them, and re-layouts  120 us (18%)
  other arithmetic  13.6 us (2%)
  starting transfers between devices  12.7 us (2%)
    all_to_all x1, waiting for transfers between devices, per_device(): lax.all_to_all(rows_done, 'space', split_axis=2, concat_axis=1, tiled=True)  180 us
    all_to_all x1, blocking collectives, per_device(): lax.all_to_all(banded, 'space', split_axis=1, concat_axis=2, tiled=True)  136 us
    dot_general x4, matrix products, below_product(): jnp.einsum('ji,bjs->bis', tile, below_data, precision=highest)  62.3 us
    ppermute x2, waiting for transfers between devices, from_behind(): lax.ppermute(value, axis, [(source, source + steps) for source in range(i...  57.7 us
    dot_general x4, matrix products, above_product(): jnp.einsum('ij,bjs->bis', tile, above_data, precision=highest)  43.5 us
    mul x3, local copies, waits for them, and re-layouts, per_device(): columns.reshape(local_blocks, HB, cell_count) * local_amp[:, None, None]  20.4 us
    unnamed x24, local copies, waits for them, and re-layouts  20 us
    dot_general x1, matrix products, per_device(): jnp.einsum('ij,hjl->hil', lat_factor, lax.all_to_all(rows_done, 'space',...  19.1 us
  transfers between devices with their start and end apart: 3, of which 2 were waited for; matrix products, arithmetic and copies ran while one was open for 9% of the time, Pallas kernels for 0%

commit v1 on v0

v1 whole, which is shorter than its diff:
```python
import functools

import jax
import jax.numpy as jnp
from jax import lax
from jax.experimental import pallas as pl
from jax.experimental.pallas import tpu as pltpu
from jax.sharding import PartitionSpec as P

F32, BF16 = jnp.float32, jnp.bfloat16
MIB = 1 << 20
CHUNKS = 2
LANES = 128


def split(x):
    high = x.astype(BF16)
    return high, (x - high.astype(F32)).astype(BF16)


def halves(x):
    high = lax.reduce_precision(x, 8, 7)
    return high.astype(BF16), lax.reduce_precision(x - high, 8, 7).astype(BF16)


def params(mib):
    return pltpu.CompilerParams(vmem_limit_bytes=mib * MIB)


def cost(flops, nbytes):
    return pl.CostEstimate(flops=int(flops), bytes_accessed=int(nbytes), transcendentals=0)


def head_kernel(lats, field_ref, mask_ref, lon_ref, out_ref, masked):
    hours = field_ref.shape[0] // lats
    cols = out_ref.shape[0] // lats
    for tile in range(masked.shape[0]):
        lanes = slice(tile * LANES, (tile + 1) * LANES)
        masked[tile] = mask_ref[:, lanes].astype(F32) * field_ref[:, lanes]
    weights = lon_ref[...]
    for i in range(lats):
        strided = pl.ds(i, hours, stride=lats)
        tiles = [masked[tile, strided, :] for tile in range(masked.shape[0])]
        high, low = split(jnp.concatenate(tiles, axis=1))
        rows = jnp.concatenate([high, low, high], axis=1)
        out_ref[pl.ds(i, cols, stride=lats), :] = lax.dot_general(
            weights, rows, (((1,), (1,)), ((), ())), preferred_element_type=F32
        )


def head(field, mask, lon3, lats, hour_block):
    rows, lon = field.shape
    hours = rows // lats
    cols = lon3.shape[0]
    return pl.pallas_call(
        functools.partial(head_kernel, lats),
        grid=(hours // hour_block,),
        in_specs=[
            pl.BlockSpec((hour_block * lats, lon), lambda t: (t, 0)),
            pl.BlockSpec((hour_block * lats, lon), lambda t: (t, 0)),
            pl.BlockSpec(lon3.shape, lambda t: (0, 0)),
        ],
        out_specs=pl.BlockSpec((cols * lats, hour_block), lambda t: (0, t)),
        out_shape=jax.ShapeDtypeStruct((cols * lats, hours), F32),
        scratch_shapes=[pltpu.VMEM((lon // LANES, hour_block * lats, LANES), F32)],
        compiler_params=params(40),
        cost_estimate=cost(6 * rows * lon * cols, 4 * rows * (2 * lon + cols)),
        name="head",
    )(field, mask, lon3)


def lat_kernel(x_ref, lat_ref, out_ref):
    parts, count, lats, hours = x_ref.shape
    weights = lat_ref[...]
    for j in range(count):
        high, low = split(x_ref[:, j].reshape(parts * lats, hours))
        rows = jnp.concatenate([high, low, high], axis=0)
        product = jnp.dot(weights, rows, preferred_element_type=F32)
        out_ref[:, j] = product.reshape(parts, lats, hours)


def lat_products(x, lat3):
    parts, count, lats, hours = x.shape
    block = min(count, 4)
    spec = pl.BlockSpec((parts, block, lats, hours), lambda j: (0, j, 0, 0))
    return pl.pallas_call(
        lat_kernel,
        grid=(count // block,),
        in_specs=[spec, pl.BlockSpec(lat3.shape, lambda j: (0, 0))],
        out_specs=spec,
        out_shape=jax.ShapeDtypeStruct(x.shape, F32),
        compiler_params=params(40),
        cost_estimate=cost(6 * x.size * parts * lats, 8 * x.size),
        name="lat",
    )(x, lat3)


def time_kernel(wide, below_ref, own_ref, above_ref, high_ref, low_ref, out_ref):
    reach = below_ref.shape[1]
    hours = own_ref.shape[1]
    padded = jnp.concatenate([below_ref[...], own_ref[...], above_ref[...]], axis=1)
    high, low = split(padded)
    for start in range(0, hours, wide):
        near = slice(start, start + wide + 2 * reach)
        columns = slice(start, start + wide)
        out_ref[:, columns] = (
            jnp.dot(high[:, near], high_ref[near, columns], preferred_element_type=F32)
            + jnp.dot(low[:, near], high_ref[near, columns], preferred_element_type=F32)
            + jnp.dot(high[:, near], low_ref[near, columns], preferred_element_type=F32)
        )


def time_products(below, own, above, high, low):
    rows, hours = own.shape
    reach = below.shape[1]
    block = min(rows, 256)
    wide = min(hours, 256)
    side = pl.BlockSpec((block, reach), lambda r: (r, 0))
    spec = pl.BlockSpec((block, hours), lambda r: (r, 0))
    whole = pl.BlockSpec(high.shape, lambda r: (0, 0))
    return pl.pallas_call(
        functools.partial(time_kernel, wide),
        grid=(rows // block,),
        in_specs=[side, spec, side, whole, whole],
        out_specs=spec,
        out_shape=jax.ShapeDtypeStruct((rows, hours), F32),
        compiler_params=params(40),
        cost_estimate=cost(6 * rows * hours * (wide + 2 * reach), 4 * rows * (2 * hours + 2 * reach)),
        name="time",
    )(below, own, above, high, low)


def band_matrix(time_tiles, amplitude, depth, first, blocks):
    offsets, hb, _ = time_tiles.shape
    reach = offsets - 1
    amp = lax.dynamic_slice_in_dim(jnp.pad(amplitude, reach), first, blocks + 2 * reach)
    dep = lax.dynamic_slice_in_dim(jnp.pad(depth, reach), first, blocks + 2 * reach)
    flipped = jnp.swapaxes(time_tiles, 1, 2)
    columns = []
    for b in range(blocks):
        own = b + reach
        tiles = []
        for r in range(blocks + 2 * reach):
            k = r - own
            if abs(k) > reach:
                tiles.append(jnp.zeros((hb, hb), F32))
                continue
            kept = (abs(k) <= dep[min(r, own)]).astype(F32)
            tile = flipped[k] if k >= 0 else time_tiles[-k]
            tiles.append((kept * amp[own] * amp[r]) * tile)
        columns.append(jnp.concatenate(tiles, axis=0))
    return halves(jnp.concatenate(columns, axis=1))


def tail_kernel(lats, z_ref, field_ref, mask_ref, noise_ref, *rest):
    out_ref, turned = rest[-2], rest[-1]
    cols = z_ref.shape[0] // lats
    hours = z_ref.shape[1]
    for i in range(lats):
        turned[pl.ds(i, hours, stride=lats), :] = z_ref[pl.ds(i, cols, stride=lats), :].T
    shape = (hours, lats, cols)
    out_ref[...] = (
        mask_ref[...].astype(F32).reshape(shape) * turned[...].reshape(shape)
        + noise_ref[...][None] * field_ref[...].reshape(shape)
    ).reshape(hours * lats, cols)


def tail(z, field, mask, noise, before, chunk, lats, hour_block):
    rows, lon = field.shape
    cols = z.shape[0] // lats
    hours = z.shape[1]
    spec = pl.BlockSpec((hour_block * lats, cols), lambda t: (t, chunk))
    operands = [z, field, mask, noise]
    in_specs = [
        pl.BlockSpec((cols * lats, hour_block), lambda t: (0, t)),
        spec,
        spec,
        pl.BlockSpec((lats, cols), lambda t: (0, chunk)),
    ]
    aliases = {}
    if before is not None:
        operands.append(before)
        in_specs.append(pl.BlockSpec(memory_space=pl.ANY))
        aliases = {4: 0}
    return pl.pallas_call(
        functools.partial(tail_kernel, lats),
        grid=(hours // hour_block,),
        in_specs=in_specs,
        out_specs=spec,
        out_shape=jax.ShapeDtypeStruct((rows, lon), F32),
        scratch_shapes=[pltpu.VMEM((hour_block * lats, cols), F32)],
        input_output_aliases=aliases,
        compiler_params=params(40),
        cost_estimate=cost(4 * rows * cols, 16 * rows * cols),
        name="tail",
    )(*operands)


def neighbour(value, steps):
    count = lax.axis_size("tm")
    pairs = [(i, i + steps) for i in range(count) if 0 <= i + steps < count]
    return lax.ppermute(value, "tm", pairs)


def per_device(field, mask, noise, lat_factor, lon_factor, time_tiles, amplitude, depth):
    hours, lats, lon = field.shape
    hb = time_tiles.shape[1]
    reach = (time_tiles.shape[0] - 1) * hb
    parts = lax.axis_size("space")
    width = lon // CHUNKS
    count = width // parts
    field = field.reshape(hours * lats, lon)
    mask = mask.reshape(hours * lats, lon)
    first = lax.axis_index("tm") * (hours // hb)
    lon_high, lon_low = halves(lon_factor)
    lat_high, lat_low = halves(lat_factor)
    lon3 = jnp.concatenate([lon_high, lon_high, lon_low], axis=1)
    lat3 = jnp.concatenate([lat_high, lat_high, lat_low], axis=1)
    band_high, band_low = band_matrix(time_tiles, amplitude, depth, first, hours // hb)
    out = None
    for chunk in range(CHUNKS):
        rows_done = head(field, mask, lon3[chunk * width : (chunk + 1) * width], lats, hb)
        rows_done = rows_done.reshape(parts, count, lats, hours)
        columns = lat_products(
            lax.all_to_all(rows_done, "space", split_axis=0, concat_axis=0, tiled=True), lat3
        ).reshape(width * lats, hours)
        below = neighbour(columns[:, hours - reach :], 1)
        above = neighbour(columns[:, :reach], -1)
        banded = time_products(below, columns, above, band_high, band_low)
        banded = lax.all_to_all(
            banded.reshape(parts, count, lats, hours), "space", split_axis=0, concat_axis=0, tiled=True
        )
        out = tail(banded.reshape(width * lats, hours), field, mask, noise, out, chunk, lats, hb)
    return out.reshape(hours, lats, lon)


def solution(mesh):
    in_specs = (
        P("tm", "space", None),
        P("tm", "space", None),
        P("space", None),
        P(),
        P(),
        P(),
        P(),
        P(),
    )
    out_specs = P("tm", "space", None)
    return jax.shard_map(
        per_device, mesh=mesh, in_specs=in_specs, out_specs=out_specs, check_vma=False
    )
```

time: 685 us -> 420 us (0.61)
  matrix products: 155 us -> 0 us
  blocking collectives: 136 us -> 0 us
  local copies, waits for them, and re-layouts: 120 us -> 24.6 us
  Pallas kernels: 0 us -> 62.9 us
  between operations: 0.57 us -> 63.4 us
  starting transfers between devices: 12.7 us -> 35.3 us
  waiting for transfers between devices: 238 us -> 220 us
    dot_general x11 -> x0, matrix products: 155 us -> none  [the longest x4 62.3 us: below_product(): jnp.einsum('ji,bjs->bis', tile, below_data, precision=highest)]
    all_to_all x1 -> x0, blocking collectives: 136 us -> none  [per_device(): lax.all_to_all(banded, 'space', split_axis=1, concat_axis=2, tiled=True)]
    pallas_call x0 -> x8, Pallas kernels: none -> 62.9 us  [the longest x2 21.7 us: time_products(): pl.pallas_call(functools.partial(time_kernel, wide), grid=(rows // block,...]
    all_to_all x1 -> x4, waiting for transfers between devices: 180 us -> 132 us  [the longest x2 74.4 us: per_device(): lax.all_to_all(rows_done, 'space', split_axis=0, concat_axis=0, tiled=True)]
    mul x4 -> x0, local copies, waits for them, and re-layouts: 32.2 us -> none  [the longest x3 20.4 us: per_device(): columns.reshape(local_blocks, HB, cell_count) * local_amp[:, None, None]]
    ppermute x2 -> x4, waiting for transfers between devices: 57.7 us -> 88.1 us  [neighbour(): return lax.ppermute(value, 'tm', pairs)]
    reshape x2 -> x0, local copies, waits for them, and re-layouts: 20.2 us -> none  [the longest x1 10.3 us: per_device(): banded = banded.reshape(hour_count, columns.shape[1], columns.shape[2])]
    all_to_all x1 -> x4, starting transfers between devices: 6.93 us -> 26.1 us  [the longest x2 13.6 us: per_device(): lax.all_to_all(rows_done, 'space', split_axis=0, concat_axis=0, tiled=True)]
  transfers between devices with their start and end apart: 3 -> 8, of which waited for: 2 -> 7; matrix products, arithmetic and copies ran while one was open for 9% -> 3% of each run, Pallas kernels for 0% -> 11%
where the time goes in v1:
time: 420 us; the launch traced here: 414 us
  waiting for transfers between devices  220 us (52%)
  between operations  63.4 us (15%)
  Pallas kernels  62.9 us (15%)
  starting transfers between devices  35.3 us (8%)
  local copies, waits for them, and re-layouts  24.6 us (6%)
  other arithmetic  8.5 us (2%)
    ppermute x4, waiting for transfers between devices, neighbour(): return lax.ppermute(value, 'tm', pairs)  88.1 us
    all_to_all x2, waiting for transfers between devices, per_device(): lax.all_to_all(rows_done, 'space', split_axis=0, concat_axis=0, tiled=True)  74.4 us
    all_to_all x2, waiting for transfers between devices, per_device(): lax.all_to_all(banded.reshape(parts, count, lats, hours), 'space', split_...  57.2 us
    unnamed x40, local copies, waits for them, and re-layouts  23 us
    pallas_call x2, Pallas kernels, time_products(): pl.pallas_call(functools.partial(time_kernel, wide), grid=(rows // block,...  21.7 us
    pallas_call x2, Pallas kernels, head(): pl.pallas_call(functools.partial(head_kernel, lats), grid=(hours // hour_...  18.8 us
    pallas_call x2, Pallas kernels, tail(): pl.pallas_call(functools.partial(tail_kernel, lats), grid=(hours // hour_...  14.3 us
    all_to_all x2, starting transfers between devices, per_device(): lax.all_to_all(rows_done, 'space', split_axis=0, concat_axis=0, tiled=True)  13.6 us
  transfers between devices with their start and end apart: 8, of which 7 were waited for; matrix products, arithmetic and copies ran while one was open for 3% of the time, Pallas kernels for 11%

profile of v1, /device:TPU:10, one launch (start us, length us, event | category | flops | bytes accessed | tf_op | source)
XLA Modules:
  0.0 414.4 jit_solution(14359548232551976227)
XLA Ops:
  0.0 1.0 reduce-precision_convert_fusion.1
  1.1 0.0 copy-start
  1.1 3.4 copy-done
  4.4 9.4 %head.3 = f32[2048,512]{1,0:T(8,128)S(1)} custom-call(f32[8192,256]{1,0:T(8,128)S(1)} %bitcast.126, s32[8192,256]{1,0:T(8,128)} %bitcast.140, bf16[128,768]{1,0:T(8,128)(2,1)S(1)} %get-tuple-element.7.lon_ref), custom_call_target="tpu_custom_call" | custom-call | flops 1610612736 | bytes 20971520 | tf_op jit(solution)/shard_map/head/pallas_call | solution.py:55
  13.8 0.0 copy-start.5
  13.8 2.0 copy-done.5
  15.8 6.4 %all-to-all-start.2 = ((f32[8,16,16,512]{3,2,1,0:T(8,128)}), f32[8,16,16,512]{3,2,1,0:T(8,128)}, u32[]{:S(2)}, u32[]{:S(2)}) async-start(f32[8,16,16,512]{3,2,1,0:T(8,128)} %bitcast.131), calls=%async_computation.2 | async-start | bytes 8388608 | tf_op jit(solution)/shard_map/all_to_all | solution.py:225
  22.2 0.0 copy-done.15
  22.2 0.1 pad_dynamic-slice_fusion
  22.3 0.0 copy-done.16
  22.3 0.1 pad_dynamic-slice_fusion.1
  22.4 0.7 fusion.7
  23.1 0.6 constant_dynamic-update-slice_fusion.43
  23.7 3.4 copy-done.1
  27.1 9.4 %head.2 = f32[2048,512]{1,0:T(8,128)S(1)} custom-call(f32[8192,256]{1,0:T(8,128)S(1)} %bitcast.127, s32[8192,256]{1,0:T(8,128)} %bitcast.141, bf16[128,768]{1,0:T(8,128)(2,1)S(1)} %get-tuple-element.8.lon_ref), custom_call_target="tpu_custom_call" | custom-call | flops 1610612736 | bytes 20971520 | tf_op jit(solution)/shard_map/head/pallas_call | solution.py:55
  36.6 0.0 copy-start.4
  36.6 2.0 copy-done.4
  38.6 0.0 copy-done.12
  38.6 74.4 %all-to-all-done.2.x_ref = f32[8,16,16,512]{3,2,1,0:T(8,128)} async-done(((f32[8,16,16,512]{3,2,1,0:T(8,128)}), f32[8,16,16,512]{3,2,1,0:T(8,128)}, u32[]{:S(2)}, u32[]{:S(2)}) %all-to-all-start.2) | async-done | bytes 4194336 | tf_op jit(solution)/shard_map/all_to_all | solution.py:225
  113.0 7.1 %all-to-all-start = ((f32[8,16,16,512]{3,2,1,0:T(8,128)}), f32[8,16,16,512]{3,2,1,0:T(8,128)}, u32[]{:S(2)}, u32[]{:S(2)}) async-start(f32[8,16,16,512]{3,2,1,0:T(8,128)} %bitcast.130), calls=%async_computation | async-start | bytes 8388608 | tf_op jit(solution)/shard_map/all_to_all | solution.py:225
  120.1 0.7 fusion.8
  182.6 0.0 copy-done.11
  182.6 0.2 copy.10
  184.1 0.7 constant_dynamic-update-slice_fusion.42
  184.8 0.7 constant_dynamic-update-slice_fusion.7
  185.5 0.7 constant_dynamic-update-slice_fusion.17
  186.2 4.1 lat.3
  190.3 0.0 copy-start.6
  190.3 1.9 collective-permute-start.3
  192.2 2.7 collective-permute-start.2
  194.9 0.6 constant_dynamic-update-slice_fusion.28
  195.5 0.6 constant_dynamic-update-slice_fusion.38
  196.2 0.6 constant_dynamic-update-slice_fusion.2
  196.9 0.6 constant_dynamic-update-slice_fusion.12
  197.5 0.6 constant_dynamic-update-slice_fusion.23
  198.2 0.6 constant_dynamic-update-slice_fusion.34
  198.8 0.6 constant_dynamic-update-slice_fusion.33
  199.5 1.6 fusion.1
  201.1 0.0 copy-done.6
  201.1 37.1 %collective-permute-done.3.above_ref = f32[2048,512]{1,0:T(8,128)S(1)} collective-permute-done((f32[2048,512]{1,0:T(8,128)S(1)}, f32[2048,512]{1,0:T(8,128)S(1)}, u32[]{:S(2)}, u32[]{:S(2)}) %collective-permute-start.3) | collective-permute-done | bytes 4194336 | tf_op jit(solution)/shard_map/ppermute | solution.py:202
  238.2 3.8 collective-permute-done.2.below_ref
  242.0 0.0 copy-done.13
  242.0 10.8 %time.3 = f32[2048,512]{1,0:T(8,128)S(1)} custom-call(f32[2048,512]{1,0:T(8,128)S(1)} %collective-permute-done.2.below_ref, f32[2048,512]{1,0:T(8,128)} %bitcast.134, f32[2048,512]{1,0:T(8,128)} %copy-done.13, bf16[1536,512]{1,0:T(8,128)(2,1)S(1)} %get-tuple-element.6.high_ref, bf16[1536,512]{1,0:T(8,128)(2,1)S(1)} %get-tuple-element.5.low_ref), custom_call_target="tpu_custom_call" | custom-call | flops 8053063680 | bytes 16777216 | tf_op jit(solution)/shard_map/time/pallas_call | solution.py:121
  252.9 0.0 copy-start.7
  252.9 2.0 copy-done.7
  254.9 0.0 all-to-all-done.x_ref
  254.9 6.0 %all-to-all-start.3 = ((f32[8,16,16,512]{3,2,1,0:T(8,128)}), f32[8,16,16,512]{3,2,1,0:T(8,128)}, u32[]{:S(2)}, u32[]{:S(2)}) async-start(f32[8,16,16,512]{3,2,1,0:T(8,128)} %bitcast.135), calls=%async_computation.3 | async-start | bytes 8388608 | tf_op jit(solution)/shard_map/all_to_all | solution.py:230
  260.9 4.1 lat.2
  265.0 0.0 copy-start.8
  265.0 1.9 collective-permute-start.1
  266.9 2.7 collective-permute-start
  269.6 43.3 %collective-permute-done.1.above_ref = f32[2048,512]{1,0:T(8,128)S(1)} collective-permute-done((f32[2048,512]{1,0:T(8,128)S(1)}, f32[2048,512]{1,0:T(8,128)S(1)}, u32[]{:S(2)}, u32[]{:S(2)}) %collective-permute-start.1) | collective-permute-done | bytes 4194336 | tf_op jit(solution)/shard_map/ppermute | solution.py:202
  312.9 3.8 collective-permute-done.below_ref
  316.8 0.0 copy-done.8
  316.8 0.0 copy-done.14
  316.8 10.8 %time.2 = f32[2048,512]{1,0:T(8,128)S(1)} custom-call(f32[2048,512]{1,0:T(8,128)S(1)} %collective-permute-done.below_ref, f32[2048,512]{1,0:T(8,128)} %bitcast.138, f32[2048,512]{1,0:T(8,128)} %copy-done.14, bf16[1536,512]{1,0:T(8,128)(2,1)S(1)} %get-tuple-element.6.high_ref, bf16[1536,512]{1,0:T(8,128)(2,1)S(1)} %get-tuple-element.5.low_ref), custom_call_target="tpu_custom_call" | custom-call | flops 8053063680 | bytes 16777216 | tf_op jit(solution)/shard_map/time/pallas_call | solution.py:121
  327.6 2.0 copy-done.9
  329.6 20.5 %all-to-all-done.3 = f32[8,16,16,512]{3,2,1,0:T(8,128)} async-done(((f32[8,16,16,512]{3,2,1,0:T(8,128)}), f32[8,16,16,512]{3,2,1,0:T(8,128)}, u32[]{:S(2)}, u32[]{:S(2)}) %all-to-all-start.3) | async-done | bytes 4194336 | tf_op jit(solution)/shard_map/all_to_all | solution.py:230
  350.1 6.5 %all-to-all-start.1 = ((f32[8,16,16,512]{3,2,1,0:T(8,128)}), f32[8,16,16,512]{3,2,1,0:T(8,128)}, u32[]{:S(2)}, u32[]{:S(2)}) async-start(f32[8,16,16,512]{3,2,1,0:T(8,128)} %bitcast.139), calls=%async_computation.1 | async-start | bytes 8388608 | tf_op jit(solution)/shard_map/all_to_all | solution.py:230
  356.6 3.4 copy-done.2
  360.0 7.1 %tail.2.rest_0_ = f32[8192,256]{1,0:T(8,128)} custom-call(f32[2048,512]{1,0:T(8,128)} %bitcast.88.z_ref, f32[8192,256]{1,0:T(8,128)S(1)} %bitcast.128, s32[8192,256]{1,0:T(8,128)} %bitcast.142, f32[16,256]{1,0:T(8,128)S(1)} %copy-done.10), custom_call_target="tpu_custom_call" | custom-call | flops 4194304 | bytes 16777216 | tf_op jit(solution)/shard_map/tail/pallas_call | solution.py:185
  367.1 36.7 %all-to-all-done.1 = f32[8,16,16,512]{3,2,1,0:T(8,128)} async-done(((f32[8,16,16,512]{3,2,1,0:T(8,128)}), f32[8,16,16,512]{3,2,1,0:T(8,128)}, u32[]{:S(2)}, u32[]{:S(2)}) %all-to-all-start.1) | async-done | bytes 4194336 | tf_op jit(solution)/shard_map/all_to_all | solution.py:230
  403.8 3.4 copy-done.3
  407.2 7.1 %tail.3 = f32[8192,256]{1,0:T(8,128)} custom-call(f32[2048,512]{1,0:T(8,128)} %bitcast.84.z_ref, f32[8192,256]{1,0:T(8,128)S(1)} %bitcast.129, s32[8192,256]{1,0:T(8,128)} %bitcast.143, f32[16,256]{1,0:T(8,128)S(1)} %copy-done.10, f32[8192,256]{1,0:T(8,128)} %tail.2.rest_0_), custom_call_target="tpu_custom_call", output_to_operand_aliasing={{}: (4, {})} | custom-call | flops 4194304 | bytes 16777216 | tf_op jit(solution)/shard_map/tail/pallas_call | solution.py:185
  (36 shorter events, 0.2 us)
Async XLA Ops:
  1.1 3.4 copy-start
  13.8 2.0 copy-start.5
  15.8 6.4 %copy-start.15 = (f32[16]{0:T(128)S(1)}, f32[16]{0:T(128)}, u32[]{:S(2)}) copy-start(f32[16]{0:T(128)} %param.14) | copy-start | bytes 196
  15.8 6.5 %copy-start.16 = (s32[16]{0:T(128)S(1)}, s32[16]{0:T(128)}, u32[]{:S(2)}) copy-start(s32[16]{0:T(128)} %param.15) | copy-start | bytes 196
  15.8 97.1 %all-to-all-start.2 = ((f32[8,16,16,512]{3,2,1,0:T(8,128)}), f32[8,16,16,512]{3,2,1,0:T(8,128)}, u32[]{:S(2)}, u32[]{:S(2)}) async-start(f32[8,16,16,512]{3,2,1,0:T(8,128)} %bitcast.131), calls=%async_computation.2 | async-start | bytes 8388608 | tf_op jit(solution)/shard_map/all_to_all | solution.py:225
  23.7 3.4 copy-start.1
  27.1 11.5 %copy-start.12 = (f32[128,128]{1,0:T(8,128)S(1)}, f32[128,128]{1,0:T(8,128)}, u32[]{:S(2)}) copy-start(f32[128,128]{1,0:T(8,128)} %param.11) | copy-start | bytes 196612
  36.6 2.0 copy-start.4
  113.0 69.7 %copy-start.11 = (f32[5,128,128]{2,1,0:T(8,128)S(1)}, f32[5,128,128]{2,1,0:T(8,128)}, u32[]{:S(2)}) copy-start(f32[5,128,128]{2,1,0:T(8,128)} %param.13) | copy-start | bytes 983044
  113.0 141.9 %all-to-all-start = ((f32[8,16,16,512]{3,2,1,0:T(8,128)}), f32[8,16,16,512]{3,2,1,0:T(8,128)}, u32[]{:S(2)}, u32[]{:S(2)}) async-start(f32[8,16,16,512]{3,2,1,0:T(8,128)} %bitcast.130), calls=%async_computation | async-start | bytes 8388608 | tf_op jit(solution)/shard_map/all_to_all | solution.py:225
  190.3 10.8 %copy-start.6 = (f32[8,16,16,512]{3,2,1,0:T(8,128)}, f32[8,16,16,512]{3,2,1,0:T(8,128)S(1)}, u32[]{:S(2)}) copy-start(f32[8,16,16,512]{3,2,1,0:T(8,128)S(1)} %lat.3) | copy-start | bytes 12582916
  190.3 47.9 %collective-permute-start.3 = (f32[2048,512]{1,0:T(8,128)S(1)}, f32[2048,512]{1,0:T(8,128)S(1)}, u32[]{:S(2)}, u32[]{:S(2)}) collective-permute-start(f32[2048,512]{1,0:T(8,128)S(1)} %bitcast.132), channel_id=1, source_target_pairs={{8,0},{16,8},{24,16},{9,1},{17,9},{25,17},{10,2},{18,10},{26,18},{... | collective-permute-start | bytes 12582920 | tf_op jit(solution)/shard_map/ppermute | solution.py:202
  192.2 49.8 %collective-permute-start.2 = (f32[2048,512]{1,0:T(8,128)S(1)}, f32[2048,512]{1,0:T(8,128)S(1)}, u32[]{:S(2)}, u32[]{:S(2)}) collective-permute-start(f32[2048,512]{1,0:T(8,128)S(1)} %bitcast.133), channel_id=1, source_target_pairs={{0,8},{8,16},{16,24},{1,9},{9,17},{17,25},{2,10},{10,18},{18,26},{... | collective-permute-start | bytes 12582920 | tf_op jit(solution)/shard_map/ppermute | solution.py:202
  238.2 3.8 copy-start.13
  252.9 2.0 copy-start.7
  254.9 95.2 %all-to-all-start.3 = ((f32[8,16,16,512]{3,2,1,0:T(8,128)}), f32[8,16,16,512]{3,2,1,0:T(8,128)}, u32[]{:S(2)}, u32[]{:S(2)}) async-start(f32[8,16,16,512]{3,2,1,0:T(8,128)} %bitcast.135), calls=%async_computation.3 | async-start | bytes 8388608 | tf_op jit(solution)/shard_map/all_to_all | solution.py:230
  265.0 51.8 %copy-start.8 = (f32[8,16,16,512]{3,2,1,0:T(8,128)}, f32[8,16,16,512]{3,2,1,0:T(8,128)S(1)}, u32[]{:S(2)}) copy-start(f32[8,16,16,512]{3,2,1,0:T(8,128)S(1)} %lat.2) | copy-start | bytes 12582916
  265.0 47.9 %collective-permute-start.1 = (f32[2048,512]{1,0:T(8,128)S(1)}, f32[2048,512]{1,0:T(8,128)S(1)}, u32[]{:S(2)}, u32[]{:S(2)}) collective-permute-start(f32[2048,512]{1,0:T(8,128)S(1)} %bitcast.136), channel_id=1, source_target_pairs={{8,0},{16,8},{24,16},{9,1},{17,9},{25,17},{10,2},{18,10},{26,18},{... | collective-permute-start | bytes 12582920 | tf_op jit(solution)/shard_map/ppermute | solution.py:202
  266.9 49.8 %collective-permute-start = (f32[2048,512]{1,0:T(8,128)S(1)}, f32[2048,512]{1,0:T(8,128)S(1)}, u32[]{:S(2)}, u32[]{:S(2)}) collective-permute-start(f32[2048,512]{1,0:T(8,128)S(1)} %bitcast.137), channel_id=1, source_target_pairs={{0,8},{8,16},{16,24},{1,9},{9,17},{17,25},{2,10},{10,18},{18,26},{... | collective-permute-start | bytes 12582920 | tf_op jit(solution)/shard_map/ppermute | solution.py:202
  312.9 3.8 copy-start.14
  327.6 2.0 copy-start.9
  350.1 6.5 %copy-start.10 = (f32[16,256]{1,0:T(8,128)S(1)}, f32[16,256]{1,0:T(8,128)}, u32[]{:S(2)}) copy-start(f32[16,256]{1,0:T(8,128)} %noise_ref.3) | copy-start | bytes 49156
  350.1 53.7 %all-to-all-start.1 = ((f32[8,16,16,512]{3,2,1,0:T(8,128)}), f32[8,16,16,512]{3,2,1,0:T(8,128)}, u32[]{:S(2)}, u32[]{:S(2)}) async-start(f32[8,16,16,512]{3,2,1,0:T(8,128)} %bitcast.139), calls=%async_computation.1 | async-start | bytes 8388608 | tf_op jit(solution)/shard_map/all_to_all | solution.py:230
  356.6 3.4 copy-start.2
  403.8 3.4 copy-start.3

commit v2 on v0

v2 whole, which is shorter than its diff:
```python
import functools

import jax
import jax.numpy as jnp
from jax import lax
from jax.experimental import pallas as pl
from jax.experimental.pallas import tpu as pltpu
from jax.sharding import PartitionSpec as P

F32, BF16 = jnp.float32, jnp.bfloat16
MIB = 1 << 20
CHUNKS = 2
LANES = 128
VMEM = 60
THERE, BACK = ("one", "all"), ("all", "one")


def split(x):
    high = x.astype(BF16)
    return high, (x - high.astype(F32)).astype(BF16)


def params(mib):
    return pltpu.CompilerParams(vmem_limit_bytes=mib * MIB)


def cost(flops, nbytes):
    return pl.CostEstimate(flops=int(flops), bytes_accessed=int(nbytes), transcendentals=0)


def pieces_of(refs):
    near, *far = refs
    return [near.at[d] for d in range(near.shape[0])] + far


def piece_specs(parts, stack, block, index):
    near = pl.BlockSpec((stack, *block), lambda *args: (0, *index(*args)))
    return [near] + [pl.BlockSpec(block, index)] * (parts - stack)


def piece_shapes(parts, stack, shape):
    near = jax.ShapeDtypeStruct((stack, *shape), F32)
    return [near] + [jax.ShapeDtypeStruct(shape, F32)] * (parts - stack)


def sizes_of(pieces):
    stack, rows, hours = pieces[0].shape
    return stack + len(pieces) - 1, stack, rows, hours


def head_kernel(lats, parts, stacks, order_ref, field_ref, mask_ref, lon_ref, *rest):
    masked, weights = rest[-2:]
    outs, used = [], 0
    for stack in stacks:
        arrays = 1 + parts - stack
        outs += pieces_of(rest[used : used + arrays])
        used += arrays
    hours = field_ref.shape[0] // lats
    count = outs[0].shape[0] // lats

    @pl.when(pl.program_id(0) == 0)
    def _():
        for k in range(len(outs)):
            start = pl.multiple_of((k // parts * parts + order_ref[k]) * count, 8)
            high, low = split(lon_ref[pl.ds(start, count), :])
            weights[k] = jnp.concatenate([high, high, low], axis=1)

    for tile in range(masked.shape[0]):
        lanes = slice(tile * LANES, (tile + 1) * LANES)
        masked[tile] = mask_ref[:, lanes].astype(F32) * field_ref[:, lanes]
    lon3 = weights[...].reshape(len(outs) * count, weights.shape[2])

    @pl.loop(0, lats, step=2, unroll=2)
    def _(i):
        lat_rows = []
        for own in (i, i + 1):
            strided = pl.ds(own, hours, stride=lats)
            tiles = [masked[tile, strided, :] for tile in range(masked.shape[0])]
            lat_rows.append(jnp.concatenate(tiles, axis=1))
        high, low = split(jnp.concatenate(lat_rows, axis=0))
        rows = jnp.concatenate([high, low, high], axis=1)
        product = lax.dot_general(lon3, rows, (((1,), (1,)), ((), ())), preferred_element_type=F32)
        for k, out_ref in enumerate(outs):
            part = product[k * count : (k + 1) * count]
            out_ref[pl.ds(i, count, stride=lats), :] = part[:, :hours]
            out_ref[pl.ds(i + 1, count, stride=lats), :] = part[:, hours:]


def head(order, stacks, field, mask, lon_factor, parts, lats, hour_block):
    rows, lon = field.shape
    hours = rows // lats
    count = lon // len(stacks) // parts
    pieces = pl.pallas_call(
        functools.partial(head_kernel, lats, parts, stacks),
        grid_spec=pltpu.PrefetchScalarGridSpec(
            num_scalar_prefetch=1,
            grid=(hours // hour_block,),
            in_specs=[
                pl.BlockSpec((hour_block * lats, lon), lambda t, order: (t, 0)),
                pl.BlockSpec((hour_block * lats, lon), lambda t, order: (t, 0)),
                pl.BlockSpec((lon, lon), lambda t, order: (0, 0)),
            ],
            out_specs=[
                spec
                for stack in stacks
                for spec in piece_specs(parts, stack, (count * lats, hour_block), lambda t, order: (0, t))
            ],
            scratch_shapes=[
                pltpu.VMEM((lon // LANES, hour_block * lats, LANES), F32),
                pltpu.VMEM((len(stacks) * parts, count, 3 * lon), BF16),
            ],
        ),
        out_shape=[
            shape for stack in stacks for shape in piece_shapes(parts, stack, (count * lats, hours))
        ],
        compiler_params=params(VMEM),
        cost_estimate=cost(6 * rows * lon * lon, 12 * rows * lon),
        name="head",
    )(order, field, mask, lon_factor)
    result = []
    for stack in stacks:
        result.append(list(pieces[: 1 + parts - stack]))
        pieces = pieces[1 + parts - stack :]
    return result


def lat_kernel(lats, came_ref, goes_ref, *refs):
    *arrays, lat_ref, out_ref, turned, weights = refs
    parts = pieces_of(arrays)
    block = out_ref.shape[1]

    @pl.when(pl.program_id(0) == 0)
    def _():
        def ordered(ref, order_ref):
            starts = [pl.multiple_of(order_ref[d] * lats, 8) for d in range(len(parts))]
            return jnp.concatenate([ref[pl.ds(start, lats), :] for start in starts], axis=0)

        turned[...] = ordered(lat_ref, came_ref).T
        high, low = split(ordered(turned, goes_ref))
        weights[...] = jnp.concatenate([high, high, low], axis=1)

    @pl.loop(0, block, unroll=2)
    def _(j):
        rows = pl.ds(pl.multiple_of(j * lats, 8), lats)
        high, low = split(jnp.concatenate([part[rows, :] for part in parts], axis=0))
        product = jnp.dot(
            weights[...], jnp.concatenate([high, low, high], axis=0), preferred_element_type=F32
        )
        out_ref[:, j] = product.reshape(len(parts), lats, product.shape[1])


def lat_products(came, goes, pieces, lat_factor, lats):
    parts, stack, rows, hours = sizes_of(pieces)
    count = rows // lats
    block = min(count, 4)
    size = parts * rows * hours
    return pl.pallas_call(
        functools.partial(lat_kernel, lats),
        grid_spec=pltpu.PrefetchScalarGridSpec(
            num_scalar_prefetch=2,
            grid=(count // block,),
            in_specs=[
                *piece_specs(parts, stack, (block * lats, hours), lambda j, *_: (j, 0)),
                pl.BlockSpec(lat_factor.shape, lambda j, *_: (0, 0)),
            ],
            out_specs=pl.BlockSpec((parts, block, lats, hours), lambda j, *_: (0, j, 0, 0)),
            scratch_shapes=[
                pltpu.VMEM(lat_factor.shape, F32),
                pltpu.VMEM((parts * lats, 3 * parts * lats), BF16),
            ],
        ),
        out_shape=jax.ShapeDtypeStruct((parts, count, lats, hours), F32),
        compiler_params=params(VMEM),
        cost_estimate=cost(6 * size * parts * lats, 8 * size),
        name="lat",
    )(came, goes, *pieces, lat_factor)


def time_kernel(
    first_ref, amplitude_ref, depth_ref, below_ref, own_ref, above_ref, tiles_ref, *rest
):
    *arrays, padded_high, padded_low, band_high, band_low = rest
    outs = pieces_of(arrays)
    rows, wide = outs[0].shape
    hb = tiles_ref.shape[1]
    reach = tiles_ref.shape[0] - 1
    steps, near, _ = band_high.shape
    pair = wide // hb
    step = pl.program_id(1)

    @pl.when((pl.program_id(0) == 0) & (step == 0))
    def _():
        band_high[...] = jnp.zeros_like(band_high)
        band_low[...] = jnp.zeros_like(band_low)

        @pl.loop(0, steps * pair)
        def _(b):
            here = first_ref[0] + b
            lane = pl.ds(pl.multiple_of(b % pair * hb, hb), hb)

            def put(k, tile):
                there = jnp.clip(here + k, 0, depth_ref.shape[0] - 1)
                kept = (there == here + k) & (abs(k) <= depth_ref[jnp.minimum(here, there)])
                weight = jnp.where(kept, amplitude_ref[here] * amplitude_ref[there], 0.0)
                high, low = split(weight * tile)
                row = pl.ds(pl.multiple_of((b % pair + reach + k) * hb, hb), hb)
                band_high[b // pair, row, lane] = high
                band_low[b // pair, row, lane] = low

            @pl.loop(0, reach + 1)
            def _(k):
                put(k, tiles_ref[k].T)

            @pl.loop(1, reach + 1)
            def _(k):
                put(-k, tiles_ref[k])

    @pl.when(step == 0)
    def _():
        sides = [ref[...].reshape(len(outs) * rows, ref.shape[3]) for ref in (below_ref, own_ref, above_ref)]
        padded_high[...], padded_low[...] = split(jnp.concatenate(sides, axis=1))

    lanes = pl.ds(pl.multiple_of(step * wide, wide), near)
    high = padded_high[:, lanes]
    product = (
        jnp.dot(high, band_high[step], preferred_element_type=F32)
        + jnp.dot(padded_low[:, lanes], band_high[step], preferred_element_type=F32)
        + jnp.dot(high, band_low[step], preferred_element_type=F32)
    )
    for d, out_ref in enumerate(outs):
        out_ref[...] = product[d * rows : (d + 1) * rows]


def time_products(stack, first, amplitude, depth, below, own, above, time_tiles):
    parts, count, lats, hours = own.shape
    reach = below.shape[3]
    block = min(count, 4)
    wide = min(hours, 2 * time_tiles.shape[1])
    near = wide + 2 * reach
    rows = parts * block * lats
    side = pl.BlockSpec((parts, block, lats, reach), lambda r, s, *_: (0, r, 0, 0))
    spec = pl.BlockSpec((parts, block, lats, hours), lambda r, s, *_: (0, r, 0, 0))
    return pl.pallas_call(
        time_kernel,
        grid_spec=pltpu.PrefetchScalarGridSpec(
            num_scalar_prefetch=3,
            grid=(count // block, hours // wide),
            in_specs=[side, spec, side, pl.BlockSpec(time_tiles.shape, lambda r, s, *_: (0, 0, 0))],
            out_specs=piece_specs(parts, stack, (block * lats, wide), lambda r, s, *_: (r, s)),
            scratch_shapes=[
                pltpu.VMEM((rows, hours + 2 * reach), BF16),
                pltpu.VMEM((rows, hours + 2 * reach), BF16),
                pltpu.VMEM((hours // wide, near, wide), BF16),
                pltpu.VMEM((hours // wide, near, wide), BF16),
            ],
        ),
        out_shape=piece_shapes(parts, stack, (count * lats, hours)),
        compiler_params=params(VMEM),
        cost_estimate=cost(6 * own.size * near, 8 * own.size + 8 * own.size // hours * reach),
        name="time",
    )(first, amplitude, depth, below, own, above, time_tiles)


def tail_kernel(lats, parts, stack, order_ref, *refs):
    arrays = 1 + parts - stack
    pieces = pieces_of(refs[:arrays])
    field_ref, mask_ref, noise_ref = refs[arrays : arrays + 3]
    out_ref, gathered, turned = refs[-3:]
    count = pieces[0].shape[0] // lats
    hours = pieces[0].shape[1]
    for i in range(lats):
        for d, piece in enumerate(pieces):
            start = pl.multiple_of((order_ref[d]) * count, 8)
            gathered[i, pl.ds(start, count), :] = piece[pl.ds(i, count, stride=lats), :]
        turned[pl.ds(i, hours, stride=lats), :] = gathered[i].T
    shape = (hours, lats, parts * count)
    out_ref[...] = (
        mask_ref[...].astype(F32).reshape(shape) * turned[...].reshape(shape)
        + noise_ref[...][None] * field_ref[...].reshape(shape)
    ).reshape(out_ref.shape)


def tail(order, pieces, field, mask, noise, before, chunk, lats, hour_block):
    rows, lon = field.shape
    parts, stack, piece_rows, hours = sizes_of(pieces)
    width = parts * piece_rows // lats
    spec = pl.BlockSpec((hour_block * lats, width), lambda t, order: (t, chunk))
    operands = [order, *pieces, field, mask, noise]
    in_specs = [
        *piece_specs(parts, stack, (piece_rows, hour_block), lambda t, order: (0, t)),
        spec,
        spec,
        pl.BlockSpec((lats, width), lambda t, order: (0, chunk)),
    ]
    aliases = {}
    if before is not None:
        aliases = {len(operands): 0}
        operands.append(before)
        in_specs.append(pl.BlockSpec(memory_space=pl.ANY))
    return pl.pallas_call(
        functools.partial(tail_kernel, lats, parts, stack),
        grid_spec=pltpu.PrefetchScalarGridSpec(
            num_scalar_prefetch=1,
            grid=(hours // hour_block,),
            in_specs=in_specs,
            out_specs=spec,
            scratch_shapes=[
                pltpu.VMEM((lats, width, hour_block), F32),
                pltpu.VMEM((hour_block * lats, width), F32),
            ],
        ),
        out_shape=jax.ShapeDtypeStruct((rows, lon), F32),
        input_output_aliases=aliases,
        compiler_params=params(VMEM),
        cost_estimate=cost(4 * rows * width, 16 * rows * width),
        name="tail",
    )(*operands)


def neighbour(value, steps):
    count = lax.axis_size("tm")
    pairs = [(i, i + steps) for i in range(count) if 0 <= i + steps < count]
    return lax.ppermute(value, "tm", pairs)


def after(value, *earlier):
    return lax.optimization_barrier((value, *earlier))[0]


def exchange(pieces):
    parts, stack, _, _ = sizes_of(pieces)
    if stack == parts:
        return [lax.all_to_all(pieces[0], "space", split_axis=0, concat_axis=0, tiled=True)]
    result = list(pieces)
    for d in reversed(range(1, parts)):
        result[d] = lax.ppermute(pieces[d], "space", [(i, i ^ d) for i in range(parts)])
    return result


def per_device(field, mask, noise, lat_factor, lon_factor, time_tiles, amplitude, depth):
    hours, lats, lon = field.shape
    hb = time_tiles.shape[1]
    reach = (time_tiles.shape[0] - 1) * hb
    parts = lax.axis_size("space")
    field = field.reshape(hours * lats, lon)
    mask = mask.reshape(hours * lats, lon)
    place = lax.axis_index("space")
    first = (lax.axis_index("tm") * (hours // hb)).astype(jnp.int32).reshape(1)
    there = [1 if name == "one" else parts for name in THERE]
    back = [1 if name == "one" else parts for name in BACK]
    order = {1: place ^ jnp.arange(parts), parts: jnp.arange(parts)}
    order = {stack: which.astype(jnp.int32) for stack, which in order.items()}
    heads = jnp.concatenate([order[stack] for stack in there])
    sent = head(heads, there, field, mask, lon_factor, parts, lats, hb)
    arrived = [exchange(sent[0])]
    for pieces in sent[1:]:
        pieces[0] = after(pieces[0], *arrived[-1][1:])
        arrived.append(exchange(pieces))
    returned = []
    for c in range(CHUNKS):
        if c > 0:
            arrived[c][0] = after(arrived[c][0], banded[0])
        columns = lat_products(order[there[c]], order[back[c]], arrived[c], lat_factor, lats)
        below = neighbour(columns[..., hours - reach :], 1)
        above = neighbour(columns[..., :reach], -1)
        banded = time_products(back[c], first, amplitude, depth, below, columns, above, time_tiles)
        returned.append(exchange(banded))
    out = None
    for c in range(CHUNKS):
        if c == 0:
            returned[c][0] = after(returned[c][0], banded[0])
        out = tail(order[back[c]], returned[c], field, mask, noise, out, c, lats, hb)
    return out.reshape(hours, lats, lon)


def solution(mesh):
    in_specs = (
        P("tm", "space", None),
        P("tm", "space", None),
        P("space", None),
        P(),
        P(),
        P(),
        P(),
        P(),
    )
    out_specs = P("tm", "space", None)
    return jax.shard_map(
        per_device, mesh=mesh, in_specs=in_specs, out_specs=out_specs, check_vma=False
    )
```

time: 685 us -> 410 us (0.60); the launches traced: 676 us -> 409 us
  matrix products: 155 us -> 0 us
  blocking collectives: 136 us -> 0 us
  local copies, waits for them, and re-layouts: 120 us -> 1.78 us
  Pallas kernels: 0 us -> 87.8 us
  waiting for transfers between devices: 238 us -> 273 us
  starting transfers between devices: 12.7 us -> 45.7 us
  other arithmetic: 13.6 us -> 0.67 us
    ppermute x2 -> x18, waiting for transfers between devices: 57.7 us -> 227 us  [the longest x14 134 us: exchange(): lax.ppermute(pieces[d], 'space', [(i, i ^ d) for i in range(parts)])]
    dot_general x11 -> x0, matrix products: 155 us -> none  [the longest x4 62.3 us: below_product(): jnp.einsum('ji,bjs->bis', tile, below_data, precision=highest)]
    all_to_all x1 -> x0, blocking collectives: 136 us -> none  [per_device(): lax.all_to_all(banded, 'space', split_axis=1, concat_axis=2, tiled=True)]
    all_to_all x1 -> x2, waiting for transfers between devices: 180 us -> 46.1 us  [exchange(): lax.all_to_all(pieces[0], 'space', split_axis=0, concat_axis=0, tiled=True)]
    pallas_call x0 -> x7, Pallas kernels: none -> 87.8 us  [the longest x2 40.2 us: time_products(): pl.pallas_call(time_kernel, grid_spec=pltpu.PrefetchScalarGridSpec(num_sc...]
    mul x4 -> x0, local copies, waits for them, and re-layouts: 32.2 us -> none  [the longest x3 20.4 us: per_device(): columns.reshape(local_blocks, HB, cell_count) * local_amp[:, None, None]]
    ppermute x2 -> x18, starting transfers between devices: 5.72 us -> 32.1 us  [the longest x14 21 us: exchange(): lax.ppermute(pieces[d], 'space', [(i, i ^ d) for i in range(parts)])]
    reshape x2 -> x0, local copies, waits for them, and re-layouts: 20.2 us -> none  [the longest x1 10.3 us: per_device(): banded = banded.reshape(hour_count, columns.shape[1], columns.shape[2])]
  transfers between devices with their start and end apart: 3 -> 20, of which waited for: 2 -> 18; matrix products, arithmetic and copies ran while one was open for 9% -> 0% of each run, Pallas kernels for 0% -> 15%
where the time goes in v2:
time: 410 us; the launch traced here: 409 us
  waiting for transfers between devices  273 us (67%)
  Pallas kernels  87.8 us (21%)
  starting transfers between devices  45.7 us (11%)
    ppermute x14, waiting for transfers between devices, exchange(): lax.ppermute(pieces[d], 'space', [(i, i ^ d) for i in range(parts)])  134 us
    ppermute x4, waiting for transfers between devices, neighbour(): return lax.ppermute(value, 'tm', pairs)  92.6 us
    all_to_all x2, waiting for transfers between devices, exchange(): lax.all_to_all(pieces[0], 'space', split_axis=0, concat_axis=0, tiled=True)  46.1 us
    pallas_call x2, Pallas kernels, time_products(): pl.pallas_call(time_kernel, grid_spec=pltpu.PrefetchScalarGridSpec(num_sc...  40.2 us
    ppermute x14, starting transfers between devices, exchange(): lax.ppermute(pieces[d], 'space', [(i, i ^ d) for i in range(parts)])  21 us
    pallas_call x2, Pallas kernels, tail(): pl.pallas_call(functools.partial(tail_kernel, lats, parts, stack), grid_s...  18.4 us
    pallas_call x1, Pallas kernels, head(): pl.pallas_call(functools.partial(head_kernel, lats, parts, stacks), grid_...  15.5 us
    pallas_call x2, Pallas kernels, lat_products(): pl.pallas_call(functools.partial(lat_kernel, lats), grid_spec=pltpu.Prefe...  13.7 us
  transfers between devices with their start and end apart: 20, of which 18 were waited for; matrix products, arithmetic and copies ran while one was open for 0% of the time, Pallas kernels for 15%

profile of v2, /device:TPU:10, one launch (start us, length us, event | category | flops | bytes accessed | tf_op | source)
XLA Modules:
  0.0 409.0 jit_solution(15827782515060405190)
XLA Ops:
  0.0 0.7 pad_add_fusion.order_ref
  0.7 15.5 %head.1 = (f32[1,256,512]{2,1,0:T(8,128)}, f32[256,512]{1,0:T(8,128)}, f32[256,512]{1,0:T(8,128)}, f32[256,512]{1,0:T(8,128)}, f32[256,512]{1,0:T(8,128)}, /*ind...) custom-call(s32[16]{0:T(128)} %pad_add_fusion.order_ref, ...), custom_call_target="tpu_custom_call" | custom-call | flops 3221225472 | bytes 25165824 | tf_op jit(solution)/shard_map/head/pallas_call | solution.py:93
  16.2 0.0 copy-done.12
  16.2 1.6 collective-permute-start
  17.8 0.4 collective-permute-start.1
  18.3 1.5 collective-permute-start.2
  19.8 2.6 collective-permute-start.3
  22.4 1.3 collective-permute-start.4
  23.7 6.8 %collective-permute-done.refs_1_ = f32[256,512]{1,0:T(8,128)S(1)} collective-permute-done((f32[256,512]{1,0:T(8,128)}, f32[256,512]{1,0:T(8,128)S(1)}, u32[]{:S(2)}, u32[]{:S(2)}) %collective-permute-start) | collective-permute-done | bytes 524320 | tf_op jit(solution)/shard_map/ppermute | solution.py:336
  30.4 1.6 collective-permute-start.5
  32.0 20.3 %collective-permute-done.1.refs_2_ = f32[256,512]{1,0:T(8,128)S(1)} collective-permute-done((f32[256,512]{1,0:T(8,128)}, f32[256,512]{1,0:T(8,128)S(1)}, u32[]{:S(2)}, u32[]{:S(2)}) %collective-permute-start.1) | collective-permute-done | bytes 524320 | tf_op jit(solution)/shard_map/ppermute | solution.py:336
  52.3 0.3 collective-permute-start.6
  52.6 9.5 %collective-permute-done.2.refs_3_ = f32[256,512]{1,0:T(8,128)S(1)} collective-permute-done((f32[256,512]{1,0:T(8,128)}, f32[256,512]{1,0:T(8,128)S(1)}, u32[]{:S(2)}, u32[]{:S(2)}) %collective-permute-start.2) | collective-permute-done | bytes 524320 | tf_op jit(solution)/shard_map/ppermute | solution.py:336
  62.1 0.0 collective-permute-done.3.refs_4_
  62.1 29.2 %collective-permute-done.4.refs_5_ = f32[256,512]{1,0:T(8,128)S(1)} collective-permute-done((f32[256,512]{1,0:T(8,128)}, f32[256,512]{1,0:T(8,128)S(1)}, u32[]{:S(2)}, u32[]{:S(2)}) %collective-permute-start.4) | collective-permute-done | bytes 524320 | tf_op jit(solution)/shard_map/ppermute | solution.py:336
  91.2 11.2 %collective-permute-done.5.refs_6_ = f32[256,512]{1,0:T(8,128)S(1)} collective-permute-done((f32[256,512]{1,0:T(8,128)}, f32[256,512]{1,0:T(8,128)S(1)}, u32[]{:S(2)}, u32[]{:S(2)}) %collective-permute-start.5) | collective-permute-done | bytes 524320 | tf_op jit(solution)/shard_map/ppermute | solution.py:336
  102.5 10.0 %collective-permute-done.6.refs_7_ = f32[256,512]{1,0:T(8,128)} collective-permute-done((f32[256,512]{1,0:T(8,128)}, f32[256,512]{1,0:T(8,128)}, u32[]{:S(2)}, u32[]{:S(2)}) %collective-permute-start.6) | collective-permute-done | bytes 524320 | tf_op jit(solution)/shard_map/ppermute | solution.py:336
  112.5 0.0 copy-done.6
  112.5 0.0 copy-done.7
  112.5 0.0 copy-done.8
  112.5 0.0 copy-done.9
  112.5 0.0 copy-done.10
  112.5 0.0 copy-done.11
  112.5 5.5 %all-to-all-start = ((f32[8,256,512]{2,1,0:T(8,128)}), f32[8,256,512]{2,1,0:T(8,128)}, u32[]{:S(2)}, u32[]{:S(2)}) async-start(f32[8,256,512]{2,1,0:T(8,128)} %get-tuple-element.33), calls=%async_computation | async-start | bytes 8388608 | tf_op jit(solution)/shard_map/all_to_all | solution.py:333
  117.9 0.6 iota.15.goes_ref
  118.5 7.0 %lat.2.own_ref = f32[8,16,16,512]{3,2,1,0:T(8,128)} custom-call(s32[8]{0:T(128)} %copy-done.12, s32[8]{0:T(128)} %iota.15.goes_ref, f32[1,256,512]{2,1,0:T(8,128)} %get-tuple-element.34.refs_0_, f32[256,512]{1,0:T(8,128)} %copy-done.6, f32[256,512]{1,0:T(8,128)} %copy-done.7, f32[256,512]{1,0:T(8,128)} %copy-done.8, f32[256,512]{1,0:T(8,128)} %copy-done.9, ...), custom_call_target="tpu_custom_call" | custom-call | flops 805306368 | bytes 8388608 | tf_op jit(solution)/shard_map/lat/pallas_call | solution.py:157
  125.6 1.9 collective-permute-start.7
  127.5 3.6 collective-permute-start.8
  131.2 44.6 %collective-permute-done.7.below_ref = f32[8,16,16,512]{3,2,1,0:T(8,128)} collective-permute-done((f32[8,16,16,512]{3,2,1,0:T(8,128)}, f32[8,16,16,512]{3,2,1,0:T(8,128)}, u32[]{:S(2)}, u32[]{:S(2)}) %collective-permute-start.7) | collective-permute-done | bytes 4194336 | tf_op jit(solution)/shard_map/ppermute | solution.py:323
  175.7 1.8 collective-permute-done.8.above_ref
  177.5 20.3 %time.2 = f32[8,256,512]{2,1,0:T(8,128)} custom-call(s32[1]{0:T(128)} %bitcast.first_ref, f32[16]{0:T(128)} %amplitude_ref.3, s32[16]{0:T(128)} %depth_ref.3, f32[8,16,16,512]{3,2,1,0:T(8,128)} %collective-permute-done.7.below_ref, f32[8,16,16,512]{3,2,1,0:T(8,128)} %lat.2.own_ref, f32[8,16,16,512]{3,2,1,0:T(8,128)} %collective-permute-done.8.above_ref, ...), custom_call_target="tpu_custom_call" | custom-call | flops 8053063680 | bytes 16777216 | tf_op jit(solution)/shard_map/time/pallas_call | solution.py:243
  197.8 9.2 %all-to-all-done.refs_0_ = f32[8,256,512]{2,1,0:T(8,128)} async-done(((f32[8,256,512]{2,1,0:T(8,128)}), f32[8,256,512]{2,1,0:T(8,128)}, u32[]{:S(2)}, u32[]{:S(2)}) %all-to-all-start) | async-done | bytes 4194336 | tf_op jit(solution)/shard_map/all_to_all | solution.py:333
  207.0 8.1 %all-to-all-start.1 = ((f32[8,256,512]{2,1,0:T(8,128)}), f32[8,256,512]{2,1,0:T(8,128)}, u32[]{:S(2)}, u32[]{:S(2)}) async-start(f32[8,256,512]{2,1,0:T(8,128)} %time.2), calls=%async_computation.1 | async-start | bytes 8388608 | tf_op jit(solution)/shard_map/all_to_all | solution.py:333
  215.1 0.6 iota.13.came_ref
  215.6 6.6 %lat.3.own_ref = f32[8,16,16,512]{3,2,1,0:T(8,128)} custom-call(s32[8]{0:T(128)} %iota.13.came_ref, s32[8]{0:T(128)} %copy-done.12, f32[8,256,512]{2,1,0:T(8,128)} %all-to-all-done.refs_0_, f32[128,128]{1,0:T(8,128)} %refs_1_.1), custom_call_target="tpu_custom_call" | custom-call | flops 805306368 | bytes 8388608 | tf_op jit(solution)/shard_map/lat/pallas_call | solution.py:157
  222.3 1.9 collective-permute-start.9
  224.2 3.6 collective-permute-start.10
  227.8 44.6 %collective-permute-done.9.below_ref = f32[8,16,16,512]{3,2,1,0:T(8,128)} collective-permute-done((f32[8,16,16,512]{3,2,1,0:T(8,128)}, f32[8,16,16,512]{3,2,1,0:T(8,128)}, u32[]{:S(2)}, u32[]{:S(2)}) %collective-permute-start.9) | collective-permute-done | bytes 4194336 | tf_op jit(solution)/shard_map/ppermute | solution.py:323
  272.4 1.8 collective-permute-done.10.above_ref
  274.1 19.9 %time.3 = (f32[1,256,512]{2,1,0:T(8,128)}, f32[256,512]{1,0:T(8,128)}, f32[256,512]{1,0:T(8,128)}, f32[256,512]{1,0:T(8,128)}, f32[256,512]{1,0:T(8,128)}, /*ind...) custom-call(s32[1]{0:T(128)} %bitcast.first_ref, f32[16]{0:T(128)} %amplitude_ref.3, s32[16]{0:T(128)} %depth_ref.3, ...), custom_call_target="tpu_custom_call" | custom-call | flops 8053063680 | bytes 16777216 | tf_op jit(solution)/shard_map/time/pallas_call | solution.py:243
  294.0 1.5 collective-permute-start.11
  295.6 0.5 collective-permute-start.12
  296.1 1.5 collective-permute-start.13
  297.6 2.4 collective-permute-start.14
  300.0 1.4 collective-permute-start.15
  301.4 4.5 %collective-permute-done.11.refs_1_ = f32[256,512]{1,0:T(8,128)S(1)} collective-permute-done((f32[256,512]{1,0:T(8,128)}, f32[256,512]{1,0:T(8,128)S(1)}, u32[]{:S(2)}, u32[]{:S(2)}) %collective-permute-start.11) | collective-permute-done | bytes 524320 | tf_op jit(solution)/shard_map/ppermute | solution.py:336
  306.0 2.9 collective-permute-start.16
  308.9 1.8 collective-permute-done.12.refs_2_
  310.6 1.5 collective-permute-start.17
  312.1 36.9 %all-to-all-done.1.refs_0_ = f32[8,256,512]{2,1,0:T(8,128)} async-done(((f32[8,256,512]{2,1,0:T(8,128)}), f32[8,256,512]{2,1,0:T(8,128)}, u32[]{:S(2)}, u32[]{:S(2)}) %all-to-all-start.1) | async-done | bytes 4194336 | tf_op jit(solution)/shard_map/all_to_all | solution.py:333
  349.1 0.6 iota.16.order_ref
  349.7 9.3 %tail.2.refs_11_ = f32[8192,256]{1,0:T(8,128)} custom-call(s32[8]{0:T(128)} %iota.16.order_ref, f32[8,256,512]{2,1,0:T(8,128)} %all-to-all-done.1.refs_0_, f32[8192,256]{1,0:T(8,128)} %bitcast.5, s32[8192,256]{1,0:T(8,128)} %bitcast.8, f32[16,256]{1,0:T(8,128)} %refs_10_.1), custom_call_target="tpu_custom_call" | custom-call | flops 4194304 | bytes 16777216 | tf_op jit(solution)/shard_map/tail/pallas_call | solution.py:300
  359.0 0.0 copy-done
  359.0 0.0 copy-done.1
  359.0 0.0 collective-permute-done.13.refs_3_
  359.0 0.0 copy-start.2
  359.0 1.3 collective-permute-done.14.refs_4_
  360.4 11.2 %collective-permute-done.15.refs_5_ = f32[256,512]{1,0:T(8,128)S(1)} collective-permute-done((f32[256,512]{1,0:T(8,128)}, f32[256,512]{1,0:T(8,128)S(1)}, u32[]{:S(2)}, u32[]{:S(2)}) %collective-permute-start.15) | collective-permute-done | bytes 524320 | tf_op jit(solution)/shard_map/ppermute | solution.py:336
  371.6 15.3 %collective-permute-done.16.refs_6_ = f32[256,512]{1,0:T(8,128)S(1)} collective-permute-done((f32[256,512]{1,0:T(8,128)}, f32[256,512]{1,0:T(8,128)S(1)}, u32[]{:S(2)}, u32[]{:S(2)}) %collective-permute-start.16) | collective-permute-done | bytes 524320 | tf_op jit(solution)/shard_map/ppermute | solution.py:336
  386.9 13.0 %collective-permute-done.17.refs_7_ = f32[256,512]{1,0:T(8,128)} collective-permute-done((f32[256,512]{1,0:T(8,128)}, f32[256,512]{1,0:T(8,128)}, u32[]{:S(2)}, u32[]{:S(2)}) %collective-permute-start.17) | collective-permute-done | bytes 524320 | tf_op jit(solution)/shard_map/ppermute | solution.py:336
  399.9 0.0 copy-done.2
  399.9 0.0 copy-done.3
  399.9 0.0 copy-done.4
  399.9 9.1 %tail.3 = f32[8192,256]{1,0:T(8,128)} custom-call(s32[8]{0:T(128)} %copy-done.12, f32[1,256,512]{2,1,0:T(8,128)} %get-tuple-element.36.refs_0_, f32[256,512]{1,0:T(8,128)} %copy-done, f32[256,512]{1,0:T(8,128)} %copy-done.1, f32[256,512]{1,0:T(8,128)} %copy-done.2, f32[256,512]{1,0:T(8,128)} %copy-done.3, ...), custom_call_target="tpu_custom_call", output_to_operand_aliasing={{}: (12, {})} | custom-call | flops 4194304 | bytes 16777216 | tf_op jit(solution)/shard_map/tail/pallas_call | solution.py:300
  (15 shorter events, 0.0 us)
Async XLA Ops:
  0.0 16.2 %copy-start.12 = (s32[8]{0:T(128)}, s32[8]{0:T(128)S(1)}, u32[]{:S(2)}) copy-start(s32[8]{0:T(128)S(1)} %iota_xor_fusion.came_ref.goes_ref.order_ref) | copy-start | bytes 100
  16.2 14.2 %collective-permute-start = (f32[256,512]{1,0:T(8,128)}, f32[256,512]{1,0:T(8,128)S(1)}, u32[]{:S(2)}, u32[]{:S(2)}) collective-permute-start(f32[256,512]{1,0:T(8,128)} %get-tuple-element.26), channel_id=1, source_target_pairs={{0,1},{1,0},{2,3},{3,2},{4,5},{5,4},{6,7},{7,6},{8,9},{9,8},{10,11... | collective-permute-start | bytes 1572872 | tf_op jit(solution)/shard_map/ppermute | solution.py:336
  17.8 34.5 %collective-permute-start.1 = (f32[256,512]{1,0:T(8,128)}, f32[256,512]{1,0:T(8,128)S(1)}, u32[]{:S(2)}, u32[]{:S(2)}) collective-permute-start(f32[256,512]{1,0:T(8,128)} %get-tuple-element.27), channel_id=1, source_target_pairs={{0,2},{1,3},{2,0},{3,1},{4,6},{5,7},{6,4},{7,5},{8,10},{9,11},{10,... | collective-permute-start | bytes 1572872 | tf_op jit(solution)/shard_map/ppermute | solution.py:336
  18.3 43.8 %collective-permute-start.2 = (f32[256,512]{1,0:T(8,128)}, f32[256,512]{1,0:T(8,128)S(1)}, u32[]{:S(2)}, u32[]{:S(2)}) collective-permute-start(f32[256,512]{1,0:T(8,128)} %get-tuple-element.28), channel_id=1, source_target_pairs={{0,3},{1,2},{2,1},{3,0},{4,7},{5,6},{6,5},{7,4},{8,11},{9,10},{10,... | collective-permute-start | bytes 1572872 | tf_op jit(solution)/shard_map/ppermute | solution.py:336
  19.8 42.3 %collective-permute-start.3 = (f32[256,512]{1,0:T(8,128)}, f32[256,512]{1,0:T(8,128)S(1)}, u32[]{:S(2)}, u32[]{:S(2)}) collective-permute-start(f32[256,512]{1,0:T(8,128)} %get-tuple-element.29), channel_id=1, source_target_pairs={{0,4},{1,5},{2,6},{3,7},{4,0},{5,1},{6,2},{7,3},{8,12},{9,13},{10,... | collective-permute-start | bytes 1572872 | tf_op jit(solution)/shard_map/ppermute | solution.py:336
  22.4 68.9 %collective-permute-start.4 = (f32[256,512]{1,0:T(8,128)}, f32[256,512]{1,0:T(8,128)S(1)}, u32[]{:S(2)}, u32[]{:S(2)}) collective-permute-start(f32[256,512]{1,0:T(8,128)} %get-tuple-element.30), channel_id=1, source_target_pairs={{0,5},{1,4},{2,7},{3,6},{4,1},{5,0},{6,3},{7,2},{8,13},{9,12},{10,... | collective-permute-start | bytes 1572872 | tf_op jit(solution)/shard_map/ppermute | solution.py:336
  30.4 82.0 %copy-start.6 = (f32[256,512]{1,0:T(8,128)}, f32[256,512]{1,0:T(8,128)S(1)}, u32[]{:S(2)}) copy-start(f32[256,512]{1,0:T(8,128)S(1)} %collective-permute-done.refs_1_) | copy-start | bytes 1572868
  30.4 72.0 %collective-permute-start.5 = (f32[256,512]{1,0:T(8,128)}, f32[256,512]{1,0:T(8,128)S(1)}, u32[]{:S(2)}, u32[]{:S(2)}) collective-permute-start(f32[256,512]{1,0:T(8,128)} %get-tuple-element.31), channel_id=1, source_target_pairs={{0,6},{1,7},{2,4},{3,5},{4,2},{5,3},{6,0},{7,1},{8,14},{9,15},{10,... | collective-permute-start | bytes 1572872 | tf_op jit(solution)/shard_map/ppermute | solution.py:336
  52.3 60.2 %copy-start.7 = (f32[256,512]{1,0:T(8,128)}, f32[256,512]{1,0:T(8,128)S(1)}, u32[]{:S(2)}) copy-start(f32[256,512]{1,0:T(8,128)S(1)} %collective-permute-done.1.refs_2_) | copy-start | bytes 1572868
  52.3 60.1 %collective-permute-start.6 = (f32[256,512]{1,0:T(8,128)}, f32[256,512]{1,0:T(8,128)}, u32[]{:S(2)}, u32[]{:S(2)}) collective-permute-start(f32[256,512]{1,0:T(8,128)} %get-tuple-element.32), channel_id=1, source_target_pairs={{0,7},{1,6},{2,5},{3,4},{4,3},{5,2},{6,1},{7,0},{8,15},{9,14},{10,... | collective-permute-start | bytes 1572872 | tf_op jit(solution)/shard_map/ppermute | solution.py:336
  62.1 50.4 %copy-start.8 = (f32[256,512]{1,0:T(8,128)}, f32[256,512]{1,0:T(8,128)S(1)}, u32[]{:S(2)}) copy-start(f32[256,512]{1,0:T(8,128)S(1)} %collective-permute-done.2.refs_3_) | copy-start | bytes 1572868
  62.1 50.4 %copy-start.9 = (f32[256,512]{1,0:T(8,128)}, f32[256,512]{1,0:T(8,128)S(1)}, u32[]{:S(2)}) copy-start(f32[256,512]{1,0:T(8,128)S(1)} %collective-permute-done.3.refs_4_) | copy-start | bytes 1572868
  91.2 21.2 %copy-start.10 = (f32[256,512]{1,0:T(8,128)}, f32[256,512]{1,0:T(8,128)S(1)}, u32[]{:S(2)}) copy-start(f32[256,512]{1,0:T(8,128)S(1)} %collective-permute-done.4.refs_5_) | copy-start | bytes 1572868
  102.5 10.0 %copy-start.11 = (f32[256,512]{1,0:T(8,128)}, f32[256,512]{1,0:T(8,128)S(1)}, u32[]{:S(2)}) copy-start(f32[256,512]{1,0:T(8,128)S(1)} %collective-permute-done.5.refs_6_) | copy-start | bytes 1572868
  112.5 94.5 %all-to-all-start = ((f32[8,256,512]{2,1,0:T(8,128)}), f32[8,256,512]{2,1,0:T(8,128)}, u32[]{:S(2)}, u32[]{:S(2)}) async-start(f32[8,256,512]{2,1,0:T(8,128)} %get-tuple-element.33), calls=%async_computation | async-start | bytes 8388608 | tf_op jit(solution)/shard_map/all_to_all | solution.py:333
  125.6 50.1 %collective-permute-start.7 = (f32[8,16,16,512]{3,2,1,0:T(8,128)}, f32[8,16,16,512]{3,2,1,0:T(8,128)}, u32[]{:S(2)}, u32[]{:S(2)}) collective-permute-start(f32[8,16,16,512]{3,2,1,0:T(8,128)} %lat.2.own_ref), channel_id=1, source_target_pairs={{0,8},{8,16},{16,24},{1,9},{9,17},{17,25},{2,10},{10,18},{18,26},{... | collective-permute-start | bytes 12582920 | tf_op jit(solution)/shard_map/ppermute | solution.py:323
  127.5 50.0 %collective-permute-start.8 = (f32[8,16,16,512]{3,2,1,0:T(8,128)}, f32[8,16,16,512]{3,2,1,0:T(8,128)}, u32[]{:S(2)}, u32[]{:S(2)}) collective-permute-start(f32[8,16,16,512]{3,2,1,0:T(8,128)} %lat.2.own_ref), channel_id=1, source_target_pairs={{8,0},{16,8},{24,16},{9,1},{17,9},{25,17},{10,2},{18,10},{26,18},{... | collective-permute-start | bytes 12582920 | tf_op jit(solution)/shard_map/ppermute | solution.py:323
  207.0 142.1 %all-to-all-start.1 = ((f32[8,256,512]{2,1,0:T(8,128)}), f32[8,256,512]{2,1,0:T(8,128)}, u32[]{:S(2)}, u32[]{:S(2)}) async-start(f32[8,256,512]{2,1,0:T(8,128)} %time.2), calls=%async_computation.1 | async-start | bytes 8388608 | tf_op jit(solution)/shard_map/all_to_all | solution.py:333
  222.3 50.1 %collective-permute-start.9 = (f32[8,16,16,512]{3,2,1,0:T(8,128)}, f32[8,16,16,512]{3,2,1,0:T(8,128)}, u32[]{:S(2)}, u32[]{:S(2)}) collective-permute-start(f32[8,16,16,512]{3,2,1,0:T(8,128)} %lat.3.own_ref), channel_id=1, source_target_pairs={{0,8},{8,16},{16,24},{1,9},{9,17},{17,25},{2,10},{10,18},{18,26},{... | collective-permute-start | bytes 12582920 | tf_op jit(solution)/shard_map/ppermute | solution.py:323
  224.2 50.0 %collective-permute-start.10 = (f32[8,16,16,512]{3,2,1,0:T(8,128)}, f32[8,16,16,512]{3,2,1,0:T(8,128)}, u32[]{:S(2)}, u32[]{:S(2)}) collective-permute-start(f32[8,16,16,512]{3,2,1,0:T(8,128)} %lat.3.own_ref), channel_id=1, source_target_pairs={{8,0},{16,8},{24,16},{9,1},{17,9},{25,17},{10,2},{18,10},{26,18},{... | collective-permute-start | bytes 12582920 | tf_op jit(solution)/shard_map/ppermute | solution.py:323
  294.0 11.9 %collective-permute-start.11 = (f32[256,512]{1,0:T(8,128)}, f32[256,512]{1,0:T(8,128)S(1)}, u32[]{:S(2)}, u32[]{:S(2)}) collective-permute-start(f32[256,512]{1,0:T(8,128)} %get-tuple-element.37), channel_id=1, source_target_pairs={{0,1},{1,0},{2,3},{3,2},{4,5},{5,4},{6,7},{7,6},{8,9},{9,8},{10,11... | collective-permute-start | bytes 1572872 | tf_op jit(solution)/shard_map/ppermute | solution.py:336
  295.6 15.1 %collective-permute-start.12 = (f32[256,512]{1,0:T(8,128)}, f32[256,512]{1,0:T(8,128)S(1)}, u32[]{:S(2)}, u32[]{:S(2)}) collective-permute-start(f32[256,512]{1,0:T(8,128)} %get-tuple-element.38), channel_id=1, source_target_pairs={{0,2},{1,3},{2,0},{3,1},{4,6},{5,7},{6,4},{7,5},{8,10},{9,11},{10,... | collective-permute-start | bytes 1572872 | tf_op jit(solution)/shard_map/ppermute | solution.py:336
  296.1 62.9 %collective-permute-start.13 = (f32[256,512]{1,0:T(8,128)}, f32[256,512]{1,0:T(8,128)S(1)}, u32[]{:S(2)}, u32[]{:S(2)}) collective-permute-start(f32[256,512]{1,0:T(8,128)} %get-tuple-element.39), channel_id=1, source_target_pairs={{0,3},{1,2},{2,1},{3,0},{4,7},{5,6},{6,5},{7,4},{8,11},{9,10},{10,... | collective-permute-start | bytes 1572872 | tf_op jit(solution)/shard_map/ppermute | solution.py:336
  297.6 62.8 %collective-permute-start.14 = (f32[256,512]{1,0:T(8,128)}, f32[256,512]{1,0:T(8,128)S(1)}, u32[]{:S(2)}, u32[]{:S(2)}) collective-permute-start(f32[256,512]{1,0:T(8,128)} %get-tuple-element.40), channel_id=1, source_target_pairs={{0,4},{1,5},{2,6},{3,7},{4,0},{5,1},{6,2},{7,3},{8,12},{9,13},{10,... | collective-permute-start | bytes 1572872 | tf_op jit(solution)/shard_map/ppermute | solution.py:336
  300.0 71.6 %collective-permute-start.15 = (f32[256,512]{1,0:T(8,128)}, f32[256,512]{1,0:T(8,128)S(1)}, u32[]{:S(2)}, u32[]{:S(2)}) collective-permute-start(f32[256,512]{1,0:T(8,128)} %get-tuple-element.41), channel_id=1, source_target_pairs={{0,5},{1,4},{2,7},{3,6},{4,1},{5,0},{6,3},{7,2},{8,13},{9,12},{10,... | collective-permute-start | bytes 1572872 | tf_op jit(solution)/shard_map/ppermute | solution.py:336
  306.0 53.0 %copy-start = (f32[256,512]{1,0:T(8,128)}, f32[256,512]{1,0:T(8,128)S(1)}, u32[]{:S(2)}) copy-start(f32[256,512]{1,0:T(8,128)S(1)} %collective-permute-done.11.refs_1_) | copy-start | bytes 1572868
  306.0 81.0 %collective-permute-start.16 = (f32[256,512]{1,0:T(8,128)}, f32[256,512]{1,0:T(8,128)S(1)}, u32[]{:S(2)}, u32[]{:S(2)}) collective-permute-start(f32[256,512]{1,0:T(8,128)} %get-tuple-element.42), channel_id=1, source_target_pairs={{0,6},{1,7},{2,4},{3,5},{4,2},{5,3},{6,0},{7,1},{8,14},{9,15},{10,... | collective-permute-start | bytes 1572872 | tf_op jit(solution)/shard_map/ppermute | solution.py:336
  310.6 48.4 %copy-start.1 = (f32[256,512]{1,0:T(8,128)}, f32[256,512]{1,0:T(8,128)S(1)}, u32[]{:S(2)}) copy-start(f32[256,512]{1,0:T(8,128)S(1)} %collective-permute-done.12.refs_2_) | copy-start | bytes 1572868
  310.6 89.3 %collective-permute-start.17 = (f32[256,512]{1,0:T(8,128)}, f32[256,512]{1,0:T(8,128)}, u32[]{:S(2)}, u32[]{:S(2)}) collective-permute-start(f32[256,512]{1,0:T(8,128)} %get-tuple-element.43), channel_id=1, source_target_pairs={{0,7},{1,6},{2,5},{3,4},{4,3},{5,2},{6,1},{7,0},{8,15},{9,14},{10,... | collective-permute-start | bytes 1572872 | tf_op jit(solution)/shard_map/ppermute | solution.py:336
  359.0 40.9 %copy-start.2 = (f32[256,512]{1,0:T(8,128)}, f32[256,512]{1,0:T(8,128)S(1)}, u32[]{:S(2)}) copy-start(f32[256,512]{1,0:T(8,128)S(1)} %collective-permute-done.13.refs_3_) | copy-start | bytes 1572868
  360.4 39.5 %copy-start.3 = (f32[256,512]{1,0:T(8,128)}, f32[256,512]{1,0:T(8,128)S(1)}, u32[]{:S(2)}) copy-start(f32[256,512]{1,0:T(8,128)S(1)} %collective-permute-done.14.refs_4_) | copy-start | bytes 1572868
  371.6 28.3 %copy-start.4 = (f32[256,512]{1,0:T(8,128)}, f32[256,512]{1,0:T(8,128)S(1)}, u32[]{:S(2)}) copy-start(f32[256,512]{1,0:T(8,128)S(1)} %collective-permute-done.15.refs_5_) | copy-start | bytes 1572868
  386.9 13.0 %copy-start.5 = (f32[256,512]{1,0:T(8,128)}, f32[256,512]{1,0:T(8,128)S(1)}, u32[]{:S(2)}) copy-start(f32[256,512]{1,0:T(8,128)S(1)} %collective-permute-done.16.refs_6_) | copy-start | bytes 1572868

commit v3 on v2

v3 whole, which is shorter than its diff:
```python
import functools

import jax
import jax.numpy as jnp
from jax import lax
from jax.experimental import pallas as pl
from jax.experimental.pallas import tpu as pltpu
from jax.sharding import PartitionSpec as P

F32, BF16 = jnp.float32, jnp.bfloat16
MIB = 1 << 20
CHUNKS = 2
LANES = 128
VMEM = 60
def sends(blocks):
    return [(0, 0, EARLY, True), (0, EARLY, blocks, False), (1, 0, blocks, True)]


EARLY = 1
RETURNS = [[True], [False]]


def split(x):
    high = x.astype(BF16)
    return high, (x - high.astype(F32)).astype(BF16)


def params(mib):
    return pltpu.CompilerParams(vmem_limit_bytes=mib * MIB)


def cost(flops, nbytes):
    return pl.CostEstimate(flops=int(flops), bytes_accessed=int(nbytes), transcendentals=0)


def pieces_of(refs, order_ref):
    if len(refs) > 1:
        return list(refs)
    return [refs[0].at[order_ref[d]] for d in range(refs[0].shape[0])]


def piece_specs(parts, stacked, block, index):
    if stacked:
        return [pl.BlockSpec((parts, *block), lambda *args: (0, *index(*args)))]
    return [pl.BlockSpec(block, index)] * parts


def piece_shapes(parts, stacked, shape):
    if stacked:
        return [jax.ShapeDtypeStruct((parts, *shape), F32)]
    return [jax.ShapeDtypeStruct(shape, F32)] * parts


def sizes_of(pieces):
    stacked = len(pieces) == 1
    return pieces[0].shape[0] if stacked else len(pieces), stacked, *pieces[0].shape[-2:]


def head_kernel(lats, order_ref, field_ref, mask_ref, lon_ref, *rest):
    masked, weights = rest[-2:]
    outs = pieces_of(rest[:-2], order_ref)
    hours = field_ref.shape[0] // lats
    count = outs[0].shape[0] // lats

    @pl.when(pl.program_id(0) == 0)
    def _():
        for d in range(len(outs)):
            start = pl.multiple_of(order_ref[d] * count, 8)
            high, low = split(lon_ref[pl.ds(start, count), :])
            weights[d] = jnp.concatenate([high, high, low], axis=1)

    for tile in range(masked.shape[0]):
        lanes = slice(tile * LANES, (tile + 1) * LANES)
        masked[tile] = mask_ref[:, lanes].astype(F32) * field_ref[:, lanes]
    lon3 = weights[...].reshape(len(outs) * count, weights.shape[2])

    @pl.loop(0, lats, step=2, unroll=2)
    def _(i):
        lat_rows = []
        for own in (i, i + 1):
            strided = pl.ds(own, hours, stride=lats)
            tiles = [masked[tile, strided, :] for tile in range(masked.shape[0])]
            lat_rows.append(jnp.concatenate(tiles, axis=1))
        high, low = split(jnp.concatenate(lat_rows, axis=0))
        rows = jnp.concatenate([high, low, high], axis=1)
        product = lax.dot_general(lon3, rows, (((1,), (1,)), ((), ())), preferred_element_type=F32)
        for d, out_ref in enumerate(outs):
            part = product[d * count : (d + 1) * count]
            out_ref[pl.ds(i, count, stride=lats), :] = part[:, :hours]
            out_ref[pl.ds(i + 1, count, stride=lats), :] = part[:, hours:]


def head(order, stacked, field, mask, lon_factor, chunk, blocks, lats, hour_block):
    first, last = blocks
    lon = field.shape[1]
    hours = (last - first) * hour_block
    parts = order.shape[0]
    width = lon // CHUNKS
    count = width // parts
    rows = hours * lats
    spec = pl.BlockSpec((hour_block * lats, lon), lambda t, order: (first + t, 0))
    return pl.pallas_call(
        functools.partial(head_kernel, lats),
        grid_spec=pltpu.PrefetchScalarGridSpec(
            num_scalar_prefetch=1,
            grid=(last - first,),
            in_specs=[spec, spec, pl.BlockSpec((width, lon), lambda t, order: (chunk, 0))],
            out_specs=piece_specs(parts, stacked, (count * lats, hour_block), lambda t, order: (0, t)),
            scratch_shapes=[
                pltpu.VMEM((lon // LANES, hour_block * lats, LANES), F32),
                pltpu.VMEM((parts, count, 3 * lon), BF16),
            ],
        ),
        out_shape=piece_shapes(parts, stacked, (count * lats, hours)),
        compiler_params=params(VMEM),
        cost_estimate=cost(6 * rows * lon * width, 4 * rows * (2 * lon + width)),
        name="head",
    )(order, field, mask, lon_factor)


def lat_kernel(lats, arrays, order_ref, *refs):
    lat_ref, out_ref, turned, weights = refs[-4:]
    sets, used = [], 0
    for some in arrays:
        sets.append(pieces_of(refs[used : used + some], order_ref))
        used += some
    parts, block = out_ref.shape[:2]

    @pl.when(pl.program_id(0) == 0)
    def _():
        def ordered(ref):
            starts = [pl.multiple_of(order_ref[d] * lats, 8) for d in range(parts)]
            return jnp.concatenate([ref[pl.ds(start, lats), :] for start in starts], axis=0)

        turned[...] = ordered(lat_ref).T
        high, low = split(ordered(turned))
        weights[...] = jnp.concatenate([high, high, low], axis=1)

    @pl.loop(0, block, unroll=2)
    def _(j):
        rows = pl.ds(pl.multiple_of(j * lats, 8), lats)
        values = [jnp.concatenate([piece[rows, :] for piece in pieces], axis=0) for pieces in sets]
        high, low = split(jnp.concatenate(values, axis=1))
        product = jnp.dot(
            weights[...], jnp.concatenate([high, low, high], axis=0), preferred_element_type=F32
        )
        out_ref[:, j] = product.reshape(parts, lats, product.shape[1])


def lat_products(order, sets, lat_factor, lats):
    parts = order.shape[0]
    sizes = [sizes_of(pieces) for pieces in sets]
    count = sizes[0][2] // lats
    hours = sum(size[3] for size in sizes)
    block = min(count, 4)
    size = parts * count * lats * hours
    return pl.pallas_call(
        functools.partial(lat_kernel, lats, [len(pieces) for pieces in sets]),
        grid_spec=pltpu.PrefetchScalarGridSpec(
            num_scalar_prefetch=1,
            grid=(count // block,),
            in_specs=[
                spec
                for _, stacked, _, some in sizes
                for spec in piece_specs(parts, stacked, (block * lats, some), lambda j, order: (j, 0))
            ]
            + [pl.BlockSpec(lat_factor.shape, lambda j, order: (0, 0))],
            out_specs=pl.BlockSpec((parts, block, lats, hours), lambda j, order: (0, j, 0, 0)),
            scratch_shapes=[
                pltpu.VMEM(lat_factor.shape, F32),
                pltpu.VMEM((parts * lats, 3 * parts * lats), BF16),
            ],
        ),
        out_shape=jax.ShapeDtypeStruct((parts, count, lats, hours), F32),
        compiler_params=params(VMEM),
        cost_estimate=cost(6 * size * parts * lats, 8 * size),
        name="lat",
    )(order, *[piece for pieces in sets for piece in pieces], lat_factor)


def time_kernel(
    arrays, order_ref, first_ref, amplitude_ref, depth_ref, below_ref, own_ref, above_ref, tiles_ref, *rest
):
    padded_high, padded_low, band_high, band_low = rest[-4:]
    sets, used = [], 0
    for some in arrays:
        sets.append(pieces_of(rest[used : used + some], order_ref))
        used += some
    parts = own_ref.shape[0]
    rows, wide = sets[0][0].shape
    hb = tiles_ref.shape[1]
    reach = tiles_ref.shape[0] - 1
    steps, near, _ = band_high.shape
    pair = wide // hb
    step = pl.program_id(1)

    @pl.when((pl.program_id(0) == 0) & (step == 0))
    def _():
        band_high[...] = jnp.zeros_like(band_high)
        band_low[...] = jnp.zeros_like(band_low)

        @pl.loop(0, steps * pair)
        def _(b):
            here = first_ref[0] + b
            lane = pl.ds(pl.multiple_of(b % pair * hb, hb), hb)

            def put(k, tile):
                there = jnp.clip(here + k, 0, depth_ref.shape[0] - 1)
                kept = (there == here + k) & (abs(k) <= depth_ref[jnp.minimum(here, there)])
                weight = jnp.where(kept, amplitude_ref[here] * amplitude_ref[there], 0.0)
                high, low = split(weight * tile)
                row = pl.ds(pl.multiple_of((b % pair + reach + k) * hb, hb), hb)
                band_high[b // pair, row, lane] = high
                band_low[b // pair, row, lane] = low

            @pl.loop(0, reach + 1)
            def _(k):
                put(k, tiles_ref[k].T)

            @pl.loop(1, reach + 1)
            def _(k):
                put(-k, tiles_ref[k])

    @pl.when(step == 0)
    def _():
        sides = [ref[...].reshape(parts * rows, ref.shape[3]) for ref in (below_ref, own_ref, above_ref)]
        padded_high[...], padded_low[...] = split(jnp.concatenate(sides, axis=1))

    lanes = pl.ds(pl.multiple_of(step * wide, wide), near)
    high = padded_high[:, lanes]
    product = (
        jnp.dot(high, band_high[step], preferred_element_type=F32)
        + jnp.dot(padded_low[:, lanes], band_high[step], preferred_element_type=F32)
        + jnp.dot(high, band_low[step], preferred_element_type=F32)
    )
    for k, outs in enumerate(sets):

        @pl.when((len(sets) == 1) | (step == k))
        def _():
            for d, out_ref in enumerate(outs):
                out_ref[...] = product[d * rows : (d + 1) * rows]


def time_products(order, stacks, first, amplitude, depth, below, own, above, time_tiles):
    parts, count, lats, hours = own.shape
    reach = below.shape[3]
    block = min(count, 4)
    wide = min(hours, 2 * time_tiles.shape[1])
    near = wide + 2 * reach
    rows = parts * block * lats
    whole = len(stacks) == 1
    side = pl.BlockSpec((parts, block, lats, reach), lambda r, s, *_: (0, r, 0, 0))
    spec = pl.BlockSpec((parts, block, lats, hours), lambda r, s, *_: (0, r, 0, 0))
    index = (lambda r, s, *_: (r, s)) if whole else (lambda r, s, *_: (r, 0))
    shape = (count * lats, hours if whole else wide)
    shapes = [piece_shapes(parts, stacked, shape) for stacked in stacks]
    results = pl.pallas_call(
        functools.partial(time_kernel, [len(some) for some in shapes]),
        grid_spec=pltpu.PrefetchScalarGridSpec(
            num_scalar_prefetch=4,
            grid=(count // block, hours // wide),
            in_specs=[side, spec, side, pl.BlockSpec(time_tiles.shape, lambda r, s, *_: (0, 0, 0))],
            out_specs=[
                out for stacked in stacks for out in piece_specs(parts, stacked, (block * lats, wide), index)
            ],
            scratch_shapes=[
                pltpu.VMEM((rows, hours + 2 * reach), BF16),
                pltpu.VMEM((rows, hours + 2 * reach), BF16),
                pltpu.VMEM((hours // wide, near, wide), BF16),
                pltpu.VMEM((hours // wide, near, wide), BF16),
            ],
        ),
        out_shape=[out for some in shapes for out in some],
        compiler_params=params(VMEM),
        cost_estimate=cost(6 * own.size * near, 8 * own.size + 8 * own.size // hours * reach),
        name="time",
    )(order, first, amplitude, depth, below, own, above, time_tiles)
    sets = []
    for some in shapes:
        sets.append(list(results[: len(some)]))
        results = results[len(some) :]
    return sets


def tail_kernel(lats, arrays, order_ref, *refs):
    pieces = pieces_of(refs[:arrays], order_ref)
    field_ref, mask_ref, noise_ref = refs[arrays : arrays + 3]
    out_ref, gathered, turned = refs[-3:]
    count = pieces[0].shape[0] // lats
    hours = pieces[0].shape[1]

    @pl.loop(0, lats, unroll=4)
    def _(i):
        for d, piece in enumerate(pieces):
            start = pl.multiple_of(order_ref[d] * count, 8)
            gathered[i, pl.ds(start, count), :] = piece[pl.ds(i, count, stride=lats), :]
        turned[pl.ds(i, hours, stride=lats), :] = gathered[i].T

    shape = (hours, lats, len(pieces) * count)
    out_ref[...] = (
        mask_ref[...].astype(F32).reshape(shape) * turned[...].reshape(shape)
        + noise_ref[...][None] * field_ref[...].reshape(shape)
    ).reshape(out_ref.shape)


def tail(order, pieces, field, mask, noise, before, chunk, first, lats, hour_block):
    rows, lon = field.shape
    parts, stacked, piece_rows, hours = sizes_of(pieces)
    width = parts * piece_rows // lats
    spec = pl.BlockSpec((hour_block * lats, width), lambda t, order: (first + t, chunk))
    operands = [order, *pieces, field, mask, noise]
    in_specs = [
        *piece_specs(parts, stacked, (piece_rows, hour_block), lambda t, order: (0, t)),
        spec,
        spec,
        pl.BlockSpec((lats, width), lambda t, order: (0, chunk)),
    ]
    aliases = {}
    if before is not None:
        aliases = {len(operands): 0}
        operands.append(before)
        in_specs.append(pl.BlockSpec(memory_space=pl.ANY))
    return pl.pallas_call(
        functools.partial(tail_kernel, lats, len(pieces)),
        grid_spec=pltpu.PrefetchScalarGridSpec(
            num_scalar_prefetch=1,
            grid=(hours // hour_block,),
            in_specs=in_specs,
            out_specs=spec,
            scratch_shapes=[
                pltpu.VMEM((lats, width, hour_block), F32),
                pltpu.VMEM((hour_block * lats, width), F32),
            ],
        ),
        out_shape=jax.ShapeDtypeStruct((rows, lon), F32),
        input_output_aliases=aliases,
        compiler_params=params(VMEM),
        cost_estimate=cost(4 * hours * lats * width, 16 * hours * lats * width),
        name="tail",
    )(*operands)


def neighbour(value, steps):
    count = lax.axis_size("tm")
    pairs = [(i, i + steps) for i in range(count) if 0 <= i + steps < count]
    return lax.ppermute(value, "tm", pairs)


def after(value, *earlier):
    return lax.optimization_barrier((value, *earlier))[0]


def exchange(pieces):
    if len(pieces) == 1:
        return [lax.all_to_all(pieces[0], "space", split_axis=0, concat_axis=0, tiled=True)]
    parts = len(pieces)
    result = list(pieces)
    for d in reversed(range(1, parts)):
        result[d] = lax.ppermute(pieces[d], "space", [(i, i ^ d) for i in range(parts)])
    return result


def per_device(field, mask, noise, lat_factor, lon_factor, time_tiles, amplitude, depth):
    hours, lats, lon = field.shape
    hb = time_tiles.shape[1]
    reach = (time_tiles.shape[0] - 1) * hb
    parts = lax.axis_size("space")
    field = field.reshape(hours * lats, lon)
    mask = mask.reshape(hours * lats, lon)
    place = lax.axis_index("space")
    first = (lax.axis_index("tm") * (hours // hb)).astype(jnp.int32).reshape(1)
    order = (place ^ jnp.arange(parts)).astype(jnp.int32)
    blocks = hours // hb
    arrived = []
    before = None
    for chunk, first_block, last_block, stacked in sends(blocks):
        part = (first_block, last_block)
        pieces = head(order, stacked, field, mask, lon_factor, chunk, part, lats, hb)
        if before is not None and stacked:
            pieces = [after(pieces[0], *before[1:])]
        before = exchange(pieces)
        arrived.append((chunk, before))
    returned = []
    banded = None
    for chunk in range(CHUNKS):
        sets = [pieces for which, pieces in arrived if which == chunk]
        if banded is not None:
            sets[0] = [after(sets[0][0], banded[0][0])] + sets[0][1:]
        columns = lat_products(order, sets, lat_factor, lats)
        below = neighbour(columns[..., hours - reach :], 1)
        above = neighbour(columns[..., :reach], -1)
        banded = time_products(
            order, RETURNS[chunk], first, amplitude, depth, below, columns, above, time_tiles
        )
        returned.append([exchange(pieces) for pieces in banded])
    out = None
    for chunk in range(CHUNKS):
        start = 0
        for pieces in returned[chunk]:
            if out is None:
                pieces = [after(pieces[0], banded[0][0])] + pieces[1:]
            out = tail(order, pieces, field, mask, noise, out, chunk, start, lats, hb)
            start += pieces[0].shape[-1] // hb
    return out.reshape(hours, lats, lon)


def solution(mesh):
    in_specs = (
        P("tm", "space", None),
        P("tm", "space", None),
        P("space", None),
        P(),
        P(),
        P(),
        P(),
        P(),
    )
    out_specs = P("tm", "space", None)
    return jax.shard_map(
        per_device, mesh=mesh, in_specs=in_specs, out_specs=out_specs, check_vma=False
    )
```

time: 410 us -> 406 us (level)
  waiting for transfers between devices: 273 us -> 250 us
  Pallas kernels: 87.8 us -> 105 us
    all_to_all x2 -> x3, waiting for transfers between devices: 46.1 us -> 19 us  [exchange(): lax.all_to_all(pieces[0], 'space', split_axis=0, concat_axis=0, tiled=True)]
    pallas_call x7 -> x9, Pallas kernels: 87.8 us -> 105 us  [the longest x2 40.2 us: time_products(): pl.pallas_call(functools.partial(time_kernel, [len(some) for some in shap...]
    ppermute x14, waiting for transfers between devices: 134 us -> 139 us  [exchange(): lax.ppermute(pieces[d], 'space', [(i, i ^ d) for i in range(parts)])]
    all_to_all x2 -> x3, starting transfers between devices: 13.6 us -> 18.8 us  [exchange(): lax.all_to_all(pieces[0], 'space', split_axis=0, concat_axis=0, tiled=True)]
  transfers between devices with their start and end apart: 20 -> 21, of which waited for: 18 -> 17; matrix products, arithmetic and copies ran while one was open for 0% -> 0% of each run, Pallas kernels for 15% -> 22%
where the time goes in v3:
time: 406 us; the launch traced here: 405 us
  waiting for transfers between devices  250 us (62%)
  Pallas kernels  105 us (26%)
  starting transfers between devices  48.8 us (12%)
    ppermute x14, waiting for transfers between devices, exchange(): lax.ppermute(pieces[d], 'space', [(i, i ^ d) for i in range(parts)])  139 us
    ppermute x4, waiting for transfers between devices, neighbour(): return lax.ppermute(value, 'tm', pairs)  91.6 us
    pallas_call x2, Pallas kernels, time_products(): pl.pallas_call(functools.partial(time_kernel, [len(some) for some in shap...  40.2 us
    pallas_call x3, Pallas kernels, head(): pl.pallas_call(functools.partial(head_kernel, lats), grid_spec=pltpu.Pref...  31.9 us
    pallas_call x2, Pallas kernels, tail(): pl.pallas_call(functools.partial(tail_kernel, lats, len(pieces)), grid_sp...  19.4 us
    all_to_all x3, waiting for transfers between devices, exchange(): lax.all_to_all(pieces[0], 'space', split_axis=0, concat_axis=0, tiled=True)  19 us
    all_to_all x3, starting transfers between devices, exchange(): lax.all_to_all(pieces[0], 'space', split_axis=0, concat_axis=0, tiled=True)  18.8 us
    ppermute x14, starting transfers between devices, exchange(): lax.ppermute(pieces[d], 'space', [(i, i ^ d) for i in range(parts)])  17.5 us
  transfers between devices with their start and end apart: 21, of which 17 were waited for; matrix products, arithmetic and copies ran while one was open for 0% of the time, Pallas kernels for 22%

profile of v3, /device:TPU:10, one launch (start us, length us, event | category | flops | bytes accessed | tf_op | source)
XLA Modules:
  0.0 405.3 jit_solution(6104376140301895473)
XLA Ops:
  0.0 0.5 iota_xor_fusion.order_ref
  0.5 6.3 %head.5 = f32[8,256,128]{2,1,0:T(8,128)} custom-call(s32[8]{0:T(128)} %iota_xor_fusion.order_ref, f32[8192,256]{1,0:T(8,128)} %bitcast.4, s32[8192,256]{1,0:T(8,128)} %bitcast.9, f32[256,256]{1,0:T(8,128)} %lon_ref.5), custom_call_target="tpu_custom_call" | custom-call | flops 402653184 | bytes 5242880 | tf_op jit(solution)/shard_map/head/pallas_call | solution.py:102
  6.9 6.3 %all-to-all-start.1 = ((f32[8,256,128]{2,1,0:T(8,128)}), f32[8,256,128]{2,1,0:T(8,128)S(1)}, u32[]{:S(2)}, u32[]{:S(2)}) async-start(f32[8,256,128]{2,1,0:T(8,128)} %head.5), calls=%async_computation.1 | async-start | bytes 2097152 | tf_op jit(solution)/shard_map/all_to_all | solution.py:355
  13.2 11.5 %head.4 = (f32[256,384]{1,0:T(8,128)}, f32[256,384]{1,0:T(8,128)}, f32[256,384]{1,0:T(8,128)}, f32[256,384]{1,0:T(8,128)}, f32[256,384]{1,0:T(8,128)}, /*index=5...) custom-call(s32[8]{0:T(128)} %iota_xor_fusion.order_ref, f32[8192,256]{1,0:T(8,128)} %bitcast.5, ...), custom_call_target="tpu_custom_call" | custom-call | flops 1207959552 | bytes 15728640 | tf_op jit(solution)/shard_map/head/pallas_call | solution.py:102
  24.6 1.5 collective-permute-start
  26.1 0.6 collective-permute-start.1
  26.7 1.5 collective-permute-start.2
  28.2 2.4 collective-permute-start.3
  30.5 1.5 collective-permute-start.4
  32.0 8.1 %collective-permute-done.refs_2_ = f32[256,384]{1,0:T(8,128)S(1)} collective-permute-done((f32[256,384]{1,0:T(8,128)}, f32[256,384]{1,0:T(8,128)S(1)}, u32[]{:S(2)}, u32[]{:S(2)}) %collective-permute-start) | collective-permute-done | bytes 393248 | tf_op jit(solution)/shard_map/ppermute | solution.py:359
  40.1 0.2 collective-permute-start.5
  40.4 12.9 %collective-permute-done.1.refs_3_ = f32[256,384]{1,0:T(8,128)S(1)} collective-permute-done((f32[256,384]{1,0:T(8,128)}, f32[256,384]{1,0:T(8,128)S(1)}, u32[]{:S(2)}, u32[]{:S(2)}) %collective-permute-start.1) | collective-permute-done | bytes 393248 | tf_op jit(solution)/shard_map/ppermute | solution.py:359
  53.3 0.0 collective-permute-start.6
  53.3 14.1 %head.3 = f32[8,256,512]{2,1,0:T(8,128)} custom-call(s32[8]{0:T(128)} %iota_xor_fusion.order_ref, f32[8192,256]{1,0:T(8,128)} %bitcast.6, s32[8192,256]{1,0:T(8,128)} %bitcast.11, f32[256,256]{1,0:T(8,128)} %lon_ref.5), custom_call_target="tpu_custom_call" | custom-call | flops 1610612736 | bytes 20971520 | tf_op jit(solution)/shard_map/head/pallas_call | solution.py:102
  67.4 0.0 copy-done.7
  67.4 0.0 copy-done.8
  67.4 0.0 collective-permute-done.2.refs_4_
  67.4 0.0 copy-start.9
  67.4 0.0 collective-permute-done.3.refs_5_
  67.4 0.0 copy-start.10
  67.4 18.6 %collective-permute-done.4.refs_6_ = f32[256,384]{1,0:T(8,128)S(1)} collective-permute-done((f32[256,384]{1,0:T(8,128)}, f32[256,384]{1,0:T(8,128)S(1)}, u32[]{:S(2)}, u32[]{:S(2)}) %collective-permute-start.4) | collective-permute-done | bytes 393248 | tf_op jit(solution)/shard_map/ppermute | solution.py:359
  86.0 11.9 %collective-permute-done.5.refs_7_ = f32[256,384]{1,0:T(8,128)S(1)} collective-permute-done((f32[256,384]{1,0:T(8,128)}, f32[256,384]{1,0:T(8,128)S(1)}, u32[]{:S(2)}, u32[]{:S(2)}) %collective-permute-start.5) | collective-permute-done | bytes 393248 | tf_op jit(solution)/shard_map/ppermute | solution.py:359
  97.9 8.0 %collective-permute-done.6.refs_8_ = f32[256,384]{1,0:T(8,128)} collective-permute-done((f32[256,384]{1,0:T(8,128)}, f32[256,384]{1,0:T(8,128)}, u32[]{:S(2)}, u32[]{:S(2)}) %collective-permute-start.6) | collective-permute-done | bytes 393248 | tf_op jit(solution)/shard_map/ppermute | solution.py:359
  105.9 0.0 all-to-all-done.1.refs_0_
  105.9 0.0 copy-done.9
  105.9 0.0 copy-done.10
  105.9 0.0 copy-done.11
  105.9 0.0 copy-done.12
  105.9 0.9 copy-done
  106.9 4.5 %all-to-all-start = ((f32[8,256,512]{2,1,0:T(8,128)}), f32[8,256,512]{2,1,0:T(8,128)}, u32[]{:S(2)}, u32[]{:S(2)}) async-start(f32[8,256,512]{2,1,0:T(8,128)} %head.3), calls=%async_computation | async-start | bytes 8388608 | tf_op jit(solution)/shard_map/all_to_all | solution.py:355
  111.4 6.7 %lat.2.own_ref = f32[8,16,16,512]{3,2,1,0:T(8,128)} custom-call(s32[8]{0:T(128)} %iota_xor_fusion.order_ref, f32[8,256,128]{2,1,0:T(8,128)} %copy-done, f32[256,384]{1,0:T(8,128)} %get-tuple-element.32.refs_1_, f32[256,384]{1,0:T(8,128)} %copy-done.7, f32[256,384]{1,0:T(8,128)} %copy-done.8, f32[256,384]{1,0:T(8,128)} %copy-done.9, f32[256,384]{1,0:T(8,128)} %copy-done.10, ...), custom_call_target="tpu_custom_call" | custom-call | flops 805306368 | bytes 8388608 | tf_op jit(solution)/shard_map/lat/pallas_call | solution.py:157
  118.1 1.9 collective-permute-start.8
  120.0 4.4 %collective-permute-start.7 = (f32[8,16,16,512]{3,2,1,0:T(8,128)}, f32[8,16,16,512]{3,2,1,0:T(8,128)}, u32[]{:S(2)}, u32[]{:S(2)}) collective-permute-start(f32[8,16,16,512]{3,2,1,0:T(8,128)} %lat.2.own_ref), channel_id=1, source_target_pairs={{0,8},{8,16},{16,24},{1,9},{9,17},{17,25},{2,10},{10,18},{18,26},{... | collective-permute-start | bytes 12582920 | tf_op jit(solution)/shard_map/ppermute | solution.py:346
  124.4 41.9 %collective-permute-done.8.above_ref = f32[8,16,16,512]{3,2,1,0:T(8,128)} collective-permute-done((f32[8,16,16,512]{3,2,1,0:T(8,128)}, f32[8,16,16,512]{3,2,1,0:T(8,128)}, u32[]{:S(2)}, u32[]{:S(2)}) %collective-permute-start.8) | collective-permute-done | bytes 4194336 | tf_op jit(solution)/shard_map/ppermute | solution.py:346
  166.3 3.8 collective-permute-done.7.below_ref
  170.1 20.3 %time.2 = f32[8,256,512]{2,1,0:T(8,128)} custom-call(s32[8]{0:T(128)} %iota_xor_fusion.order_ref, s32[1]{0:T(128)} %bitcast.first_ref, f32[16]{0:T(128)} %amplitude_ref.3, s32[16]{0:T(128)} %depth_ref.3, f32[8,16,16,512]{3,2,1,0:T(8,128)} %collective-permute-done.7.below_ref, f32[8,16,16,512]{3,2,1,0:T(8,128)} %lat.2.own_ref, ...), custom_call_target="tpu_custom_call" | custom-call | flops 8053063680 | bytes 16777216 | tf_op jit(solution)/shard_map/time/pallas_call | solution.py:257
  190.5 10.7 %all-to-all-done.refs_0_ = f32[8,256,512]{2,1,0:T(8,128)} async-done(((f32[8,256,512]{2,1,0:T(8,128)}), f32[8,256,512]{2,1,0:T(8,128)}, u32[]{:S(2)}, u32[]{:S(2)}) %all-to-all-start) | async-done | bytes 4194336 | tf_op jit(solution)/shard_map/all_to_all | solution.py:355
  201.1 8.0 %all-to-all-start.2 = ((f32[8,256,512]{2,1,0:T(8,128)}), f32[8,256,512]{2,1,0:T(8,128)}, u32[]{:S(2)}, u32[]{:S(2)}) async-start(f32[8,256,512]{2,1,0:T(8,128)} %time.2), calls=%async_computation.2 | async-start | bytes 8388608 | tf_op jit(solution)/shard_map/all_to_all | solution.py:355
  209.2 6.6 %lat.3.own_ref = f32[8,16,16,512]{3,2,1,0:T(8,128)} custom-call(s32[8]{0:T(128)} %iota_xor_fusion.order_ref, f32[8,256,512]{2,1,0:T(8,128)} %all-to-all-done.refs_0_, f32[128,128]{1,0:T(8,128)} %refs_1_.1), custom_call_target="tpu_custom_call" | custom-call | flops 805306368 | bytes 8388608 | tf_op jit(solution)/shard_map/lat/pallas_call | solution.py:157
  215.8 1.9 collective-permute-start.10
  217.7 4.3 %collective-permute-start.9 = (f32[8,16,16,512]{3,2,1,0:T(8,128)}, f32[8,16,16,512]{3,2,1,0:T(8,128)}, u32[]{:S(2)}, u32[]{:S(2)}) collective-permute-start(f32[8,16,16,512]{3,2,1,0:T(8,128)} %lat.3.own_ref), channel_id=1, source_target_pairs={{0,8},{8,16},{16,24},{1,9},{9,17},{17,25},{2,10},{10,18},{18,26},{... | collective-permute-start | bytes 12582920 | tf_op jit(solution)/shard_map/ppermute | solution.py:346
  222.0 42.0 %collective-permute-done.10.above_ref = f32[8,16,16,512]{3,2,1,0:T(8,128)} collective-permute-done((f32[8,16,16,512]{3,2,1,0:T(8,128)}, f32[8,16,16,512]{3,2,1,0:T(8,128)}, u32[]{:S(2)}, u32[]{:S(2)}) %collective-permute-start.10) | collective-permute-done | bytes 4194336 | tf_op jit(solution)/shard_map/ppermute | solution.py:346
  264.0 3.8 collective-permute-done.9.below_ref
  267.9 19.9 %time.3 = (f32[256,512]{1,0:T(8,128)}, f32[256,512]{1,0:T(8,128)}, f32[256,512]{1,0:T(8,128)}, f32[256,512]{1,0:T(8,128)}, f32[256,512]{1,0:T(8,128)}, /*index=5...) custom-call(s32[8]{0:T(128)} %iota_xor_fusion.order_ref, s32[1]{0:T(128)} %bitcast.first_ref, f32[16]{0:T(128)} %amplitude_ref.3, ...), custom_call_target="tpu_custom_call" | custom-call | flops 8053063680 | bytes 16777216 | tf_op jit(solution)/shard_map/time/pallas_call | solution.py:257
  287.8 1.5 collective-permute-start.11
  289.3 0.5 collective-permute-start.12
  289.8 1.5 collective-permute-start.13
  291.3 2.4 collective-permute-start.14
  293.7 1.4 collective-permute-start.15
  295.1 6.6 %collective-permute-done.11.refs_1_ = f32[256,512]{1,0:T(8,128)S(1)} collective-permute-done((f32[256,512]{1,0:T(8,128)}, f32[256,512]{1,0:T(8,128)S(1)}, u32[]{:S(2)}, u32[]{:S(2)}) %collective-permute-start.11) | collective-permute-done | bytes 524320 | tf_op jit(solution)/shard_map/ppermute | solution.py:359
  301.8 0.5 collective-permute-start.16
  302.3 2.1 collective-permute-done.12.refs_2_
  304.3 2.0 collective-permute-start.17
  306.3 8.3 %all-to-all-done.2.refs_0_ = f32[8,256,512]{2,1,0:T(8,128)} async-done(((f32[8,256,512]{2,1,0:T(8,128)}), f32[8,256,512]{2,1,0:T(8,128)}, u32[]{:S(2)}, u32[]{:S(2)}) %all-to-all-start.2) | async-done | bytes 4194336 | tf_op jit(solution)/shard_map/all_to_all | solution.py:355
  314.7 9.8 %tail.2.refs_11_ = f32[8192,256]{1,0:T(8,128)} custom-call(s32[8]{0:T(128)} %iota_xor_fusion.order_ref, f32[8,256,512]{2,1,0:T(8,128)} %all-to-all-done.2.refs_0_, f32[8192,256]{1,0:T(8,128)} %bitcast.7, s32[8192,256]{1,0:T(8,128)} %bitcast.12, f32[16,256]{1,0:T(8,128)} %refs_10_.1), custom_call_target="tpu_custom_call" | custom-call | flops 4194304 | bytes 16777216 | tf_op jit(solution)/shard_map/tail/pallas_call | solution.py:323
  324.5 0.0 copy-done.1
  324.5 0.0 copy-done.2
  324.5 0.0 collective-permute-done.13.refs_3_
  324.5 31.7 %collective-permute-done.14.refs_4_ = f32[256,512]{1,0:T(8,128)S(1)} collective-permute-done((f32[256,512]{1,0:T(8,128)}, f32[256,512]{1,0:T(8,128)S(1)}, u32[]{:S(2)}, u32[]{:S(2)}) %collective-permute-start.14) | collective-permute-done | bytes 524320 | tf_op jit(solution)/shard_map/ppermute | solution.py:359
  356.2 11.2 %collective-permute-done.15.refs_5_ = f32[256,512]{1,0:T(8,128)S(1)} collective-permute-done((f32[256,512]{1,0:T(8,128)}, f32[256,512]{1,0:T(8,128)S(1)}, u32[]{:S(2)}, u32[]{:S(2)}) %collective-permute-start.15) | collective-permute-done | bytes 524320 | tf_op jit(solution)/shard_map/ppermute | solution.py:359
  367.4 13.6 %collective-permute-done.16.refs_6_ = f32[256,512]{1,0:T(8,128)S(1)} collective-permute-done((f32[256,512]{1,0:T(8,128)}, f32[256,512]{1,0:T(8,128)S(1)}, u32[]{:S(2)}, u32[]{:S(2)}) %collective-permute-start.16) | collective-permute-done | bytes 524320 | tf_op jit(solution)/shard_map/ppermute | solution.py:359
  381.0 14.7 %collective-permute-done.17.refs_7_ = f32[256,512]{1,0:T(8,128)} collective-permute-done((f32[256,512]{1,0:T(8,128)}, f32[256,512]{1,0:T(8,128)}, u32[]{:S(2)}, u32[]{:S(2)}) %collective-permute-start.17) | collective-permute-done | bytes 524320 | tf_op jit(solution)/shard_map/ppermute | solution.py:359
  395.7 0.0 copy-done.4
  395.7 9.6 %tail.3 = f32[8192,256]{1,0:T(8,128)} custom-call(s32[8]{0:T(128)} %iota_xor_fusion.order_ref, f32[256,512]{1,0:T(8,128)} %get-tuple-element.34.refs_0_, f32[256,512]{1,0:T(8,128)} %copy-done.1, f32[256,512]{1,0:T(8,128)} %copy-done.2, f32[256,512]{1,0:T(8,128)} %copy-done.3, f32[256,512]{1,0:T(8,128)} %copy-done.4, ...), custom_call_target="tpu_custom_call", output_to_operand_aliasing={{}: (12, {})} | custom-call | flops 4194304 | bytes 16777216 | tf_op jit(solution)/shard_map/tail/pallas_call | solution.py:323
  (14 shorter events, 0.0 us)
Async XLA Ops:
  6.9 99.0 %all-to-all-start.1 = ((f32[8,256,128]{2,1,0:T(8,128)}), f32[8,256,128]{2,1,0:T(8,128)S(1)}, u32[]{:S(2)}, u32[]{:S(2)}) async-start(f32[8,256,128]{2,1,0:T(8,128)} %head.5), calls=%async_computation.1 | async-start | bytes 2097152 | tf_op jit(solution)/shard_map/all_to_all | solution.py:355
  24.6 15.5 %collective-permute-start = (f32[256,384]{1,0:T(8,128)}, f32[256,384]{1,0:T(8,128)S(1)}, u32[]{:S(2)}, u32[]{:S(2)}) collective-permute-start(f32[256,384]{1,0:T(8,128)} %get-tuple-element.24), channel_id=1, source_target_pairs={{0,1},{1,0},{2,3},{3,2},{4,5},{5,4},{6,7},{7,6},{8,9},{9,8},{10,11... | collective-permute-start | bytes 1179656 | tf_op jit(solution)/shard_map/ppermute | solution.py:359
  26.1 27.1 %collective-permute-start.1 = (f32[256,384]{1,0:T(8,128)}, f32[256,384]{1,0:T(8,128)S(1)}, u32[]{:S(2)}, u32[]{:S(2)}) collective-permute-start(f32[256,384]{1,0:T(8,128)} %get-tuple-element.25), channel_id=1, source_target_pairs={{0,2},{1,3},{2,0},{3,1},{4,6},{5,7},{6,4},{7,5},{8,10},{9,11},{10,... | collective-permute-start | bytes 1179656 | tf_op jit(solution)/shard_map/ppermute | solution.py:359
  26.7 40.7 %collective-permute-start.2 = (f32[256,384]{1,0:T(8,128)}, f32[256,384]{1,0:T(8,128)S(1)}, u32[]{:S(2)}, u32[]{:S(2)}) collective-permute-start(f32[256,384]{1,0:T(8,128)} %get-tuple-element.26), channel_id=1, source_target_pairs={{0,3},{1,2},{2,1},{3,0},{4,7},{5,6},{6,5},{7,4},{8,11},{9,10},{10,... | collective-permute-start | bytes 1179656 | tf_op jit(solution)/shard_map/ppermute | solution.py:359
  28.2 39.2 %collective-permute-start.3 = (f32[256,384]{1,0:T(8,128)}, f32[256,384]{1,0:T(8,128)S(1)}, u32[]{:S(2)}, u32[]{:S(2)}) collective-permute-start(f32[256,384]{1,0:T(8,128)} %get-tuple-element.27), channel_id=1, source_target_pairs={{0,4},{1,5},{2,6},{3,7},{4,0},{5,1},{6,2},{7,3},{8,12},{9,13},{10,... | collective-permute-start | bytes 1179656 | tf_op jit(solution)/shard_map/ppermute | solution.py:359
  30.5 55.5 %collective-permute-start.4 = (f32[256,384]{1,0:T(8,128)}, f32[256,384]{1,0:T(8,128)S(1)}, u32[]{:S(2)}, u32[]{:S(2)}) collective-permute-start(f32[256,384]{1,0:T(8,128)} %get-tuple-element.28), channel_id=1, source_target_pairs={{0,5},{1,4},{2,7},{3,6},{4,1},{5,0},{6,3},{7,2},{8,13},{9,12},{10,... | collective-permute-start | bytes 1179656 | tf_op jit(solution)/shard_map/ppermute | solution.py:359
  40.1 27.2 %copy-start.7 = (f32[256,384]{1,0:T(8,128)}, f32[256,384]{1,0:T(8,128)S(1)}, u32[]{:S(2)}) copy-start(f32[256,384]{1,0:T(8,128)S(1)} %collective-permute-done.refs_2_) | copy-start | bytes 1179652
  40.1 57.8 %collective-permute-start.5 = (f32[256,384]{1,0:T(8,128)}, f32[256,384]{1,0:T(8,128)S(1)}, u32[]{:S(2)}, u32[]{:S(2)}) collective-permute-start(f32[256,384]{1,0:T(8,128)} %get-tuple-element.29), channel_id=1, source_target_pairs={{0,6},{1,7},{2,4},{3,5},{4,2},{5,3},{6,0},{7,1},{8,14},{9,15},{10,... | collective-permute-start | bytes 1179656 | tf_op jit(solution)/shard_map/ppermute | solution.py:359
  53.3 14.1 %copy-start.8 = (f32[256,384]{1,0:T(8,128)}, f32[256,384]{1,0:T(8,128)S(1)}, u32[]{:S(2)}) copy-start(f32[256,384]{1,0:T(8,128)S(1)} %collective-permute-done.1.refs_3_) | copy-start | bytes 1179652
  53.3 52.6 %collective-permute-start.6 = (f32[256,384]{1,0:T(8,128)}, f32[256,384]{1,0:T(8,128)}, u32[]{:S(2)}, u32[]{:S(2)}) collective-permute-start(f32[256,384]{1,0:T(8,128)} %get-tuple-element.30), channel_id=1, source_target_pairs={{0,7},{1,6},{2,5},{3,4},{4,3},{5,2},{6,1},{7,0},{8,15},{9,14},{10,... | collective-permute-start | bytes 1179656 | tf_op jit(solution)/shard_map/ppermute | solution.py:359
  67.4 38.5 %copy-start.9 = (f32[256,384]{1,0:T(8,128)}, f32[256,384]{1,0:T(8,128)S(1)}, u32[]{:S(2)}) copy-start(f32[256,384]{1,0:T(8,128)S(1)} %collective-permute-done.2.refs_4_) | copy-start | bytes 1179652
  67.4 38.5 %copy-start.10 = (f32[256,384]{1,0:T(8,128)}, f32[256,384]{1,0:T(8,128)S(1)}, u32[]{:S(2)}) copy-start(f32[256,384]{1,0:T(8,128)S(1)} %collective-permute-done.3.refs_5_) | copy-start | bytes 1179652
  86.0 19.9 %copy-start.11 = (f32[256,384]{1,0:T(8,128)}, f32[256,384]{1,0:T(8,128)S(1)}, u32[]{:S(2)}) copy-start(f32[256,384]{1,0:T(8,128)S(1)} %collective-permute-done.4.refs_6_) | copy-start | bytes 1179652
  97.9 8.0 %copy-start.12 = (f32[256,384]{1,0:T(8,128)}, f32[256,384]{1,0:T(8,128)S(1)}, u32[]{:S(2)}) copy-start(f32[256,384]{1,0:T(8,128)S(1)} %collective-permute-done.5.refs_7_) | copy-start | bytes 1179652
  105.9 1.0 copy-start
  106.9 94.3 %all-to-all-start = ((f32[8,256,512]{2,1,0:T(8,128)}), f32[8,256,512]{2,1,0:T(8,128)}, u32[]{:S(2)}, u32[]{:S(2)}) async-start(f32[8,256,512]{2,1,0:T(8,128)} %head.3), calls=%async_computation | async-start | bytes 8388608 | tf_op jit(solution)/shard_map/all_to_all | solution.py:355
  118.1 48.2 %collective-permute-start.8 = (f32[8,16,16,512]{3,2,1,0:T(8,128)}, f32[8,16,16,512]{3,2,1,0:T(8,128)}, u32[]{:S(2)}, u32[]{:S(2)}) collective-permute-start(f32[8,16,16,512]{3,2,1,0:T(8,128)} %lat.2.own_ref), channel_id=1, source_target_pairs={{8,0},{16,8},{24,16},{9,1},{17,9},{25,17},{10,2},{18,10},{26,18},{... | collective-permute-start | bytes 12582920 | tf_op jit(solution)/shard_map/ppermute | solution.py:346
  120.0 50.1 %collective-permute-start.7 = (f32[8,16,16,512]{3,2,1,0:T(8,128)}, f32[8,16,16,512]{3,2,1,0:T(8,128)}, u32[]{:S(2)}, u32[]{:S(2)}) collective-permute-start(f32[8,16,16,512]{3,2,1,0:T(8,128)} %lat.2.own_ref), channel_id=1, source_target_pairs={{0,8},{8,16},{16,24},{1,9},{9,17},{17,25},{2,10},{10,18},{18,26},{... | collective-permute-start | bytes 12582920 | tf_op jit(solution)/shard_map/ppermute | solution.py:346
  201.1 113.5 %all-to-all-start.2 = ((f32[8,256,512]{2,1,0:T(8,128)}), f32[8,256,512]{2,1,0:T(8,128)}, u32[]{:S(2)}, u32[]{:S(2)}) async-start(f32[8,256,512]{2,1,0:T(8,128)} %time.2), calls=%async_computation.2 | async-start | bytes 8388608 | tf_op jit(solution)/shard_map/all_to_all | solution.py:355
  215.8 48.2 %collective-permute-start.10 = (f32[8,16,16,512]{3,2,1,0:T(8,128)}, f32[8,16,16,512]{3,2,1,0:T(8,128)}, u32[]{:S(2)}, u32[]{:S(2)}) collective-permute-start(f32[8,16,16,512]{3,2,1,0:T(8,128)} %lat.3.own_ref), channel_id=1, source_target_pairs={{8,0},{16,8},{24,16},{9,1},{17,9},{25,17},{10,2},{18,10},{26,18},{... | collective-permute-start | bytes 12582920 | tf_op jit(solution)/shard_map/ppermute | solution.py:346
  217.7 50.1 %collective-permute-start.9 = (f32[8,16,16,512]{3,2,1,0:T(8,128)}, f32[8,16,16,512]{3,2,1,0:T(8,128)}, u32[]{:S(2)}, u32[]{:S(2)}) collective-permute-start(f32[8,16,16,512]{3,2,1,0:T(8,128)} %lat.3.own_ref), channel_id=1, source_target_pairs={{0,8},{8,16},{16,24},{1,9},{9,17},{17,25},{2,10},{10,18},{18,26},{... | collective-permute-start | bytes 12582920 | tf_op jit(solution)/shard_map/ppermute | solution.py:346
  287.8 14.0 %collective-permute-start.11 = (f32[256,512]{1,0:T(8,128)}, f32[256,512]{1,0:T(8,128)S(1)}, u32[]{:S(2)}, u32[]{:S(2)}) collective-permute-start(f32[256,512]{1,0:T(8,128)} %get-tuple-element.35), channel_id=1, source_target_pairs={{0,1},{1,0},{2,3},{3,2},{4,5},{5,4},{6,7},{7,6},{8,9},{9,8},{10,11... | collective-permute-start | bytes 1572872 | tf_op jit(solution)/shard_map/ppermute | solution.py:359
  289.3 15.1 %collective-permute-start.12 = (f32[256,512]{1,0:T(8,128)}, f32[256,512]{1,0:T(8,128)S(1)}, u32[]{:S(2)}, u32[]{:S(2)}) collective-permute-start(f32[256,512]{1,0:T(8,128)} %get-tuple-element.36), channel_id=1, source_target_pairs={{0,2},{1,3},{2,0},{3,1},{4,6},{5,7},{6,4},{7,5},{8,10},{9,11},{10,... | collective-permute-start | bytes 1572872 | tf_op jit(solution)/shard_map/ppermute | solution.py:359
  289.8 34.7 %collective-permute-start.13 = (f32[256,512]{1,0:T(8,128)}, f32[256,512]{1,0:T(8,128)S(1)}, u32[]{:S(2)}, u32[]{:S(2)}) collective-permute-start(f32[256,512]{1,0:T(8,128)} %get-tuple-element.37), channel_id=1, source_target_pairs={{0,3},{1,2},{2,1},{3,0},{4,7},{5,6},{6,5},{7,4},{8,11},{9,10},{10,... | collective-permute-start | bytes 1572872 | tf_op jit(solution)/shard_map/ppermute | solution.py:359
  291.3 64.9 %collective-permute-start.14 = (f32[256,512]{1,0:T(8,128)}, f32[256,512]{1,0:T(8,128)S(1)}, u32[]{:S(2)}, u32[]{:S(2)}) collective-permute-start(f32[256,512]{1,0:T(8,128)} %get-tuple-element.38), channel_id=1, source_target_pairs={{0,4},{1,5},{2,6},{3,7},{4,0},{5,1},{6,2},{7,3},{8,12},{9,13},{10,... | collective-permute-start | bytes 1572872 | tf_op jit(solution)/shard_map/ppermute | solution.py:359
  293.7 73.7 %collective-permute-start.15 = (f32[256,512]{1,0:T(8,128)}, f32[256,512]{1,0:T(8,128)S(1)}, u32[]{:S(2)}, u32[]{:S(2)}) collective-permute-start(f32[256,512]{1,0:T(8,128)} %get-tuple-element.39), channel_id=1, source_target_pairs={{0,5},{1,4},{2,7},{3,6},{4,1},{5,0},{6,3},{7,2},{8,13},{9,12},{10,... | collective-permute-start | bytes 1572872 | tf_op jit(solution)/shard_map/ppermute | solution.py:359
  301.8 22.7 %copy-start.1 = (f32[256,512]{1,0:T(8,128)}, f32[256,512]{1,0:T(8,128)S(1)}, u32[]{:S(2)}) copy-start(f32[256,512]{1,0:T(8,128)S(1)} %collective-permute-done.11.refs_1_) | copy-start | bytes 1572868
  301.8 79.3 %collective-permute-start.16 = (f32[256,512]{1,0:T(8,128)}, f32[256,512]{1,0:T(8,128)S(1)}, u32[]{:S(2)}, u32[]{:S(2)}) collective-permute-start(f32[256,512]{1,0:T(8,128)} %get-tuple-element.40), channel_id=1, source_target_pairs={{0,6},{1,7},{2,4},{3,5},{4,2},{5,3},{6,0},{7,1},{8,14},{9,15},{10,... | collective-permute-start | bytes 1572872 | tf_op jit(solution)/shard_map/ppermute | solution.py:359
  304.3 20.1 %copy-start.2 = (f32[256,512]{1,0:T(8,128)}, f32[256,512]{1,0:T(8,128)S(1)}, u32[]{:S(2)}) copy-start(f32[256,512]{1,0:T(8,128)S(1)} %collective-permute-done.12.refs_2_) | copy-start | bytes 1572868
  304.3 91.3 %collective-permute-start.17 = (f32[256,512]{1,0:T(8,128)}, f32[256,512]{1,0:T(8,128)}, u32[]{:S(2)}, u32[]{:S(2)}) collective-permute-start(f32[256,512]{1,0:T(8,128)} %get-tuple-element.41), channel_id=1, source_target_pairs={{0,7},{1,6},{2,5},{3,4},{4,3},{5,2},{6,1},{7,0},{8,15},{9,14},{10,... | collective-permute-start | bytes 1572872 | tf_op jit(solution)/shard_map/ppermute | solution.py:359
  324.5 71.2 %copy-start.3 = (f32[256,512]{1,0:T(8,128)}, f32[256,512]{1,0:T(8,128)S(1)}, u32[]{:S(2)}) copy-start(f32[256,512]{1,0:T(8,128)S(1)} %collective-permute-done.13.refs_3_) | copy-start | bytes 1572868
  356.2 39.5 %copy-start.4 = (f32[256,512]{1,0:T(8,128)}, f32[256,512]{1,0:T(8,128)S(1)}, u32[]{:S(2)}) copy-start(f32[256,512]{1,0:T(8,128)S(1)} %collective-permute-done.14.refs_4_) | copy-start | bytes 1572868
  367.4 28.3 %copy-start.5 = (f32[256,512]{1,0:T(8,128)}, f32[256,512]{1,0:T(8,128)S(1)}, u32[]{:S(2)}) copy-start(f32[256,512]{1,0:T(8,128)S(1)} %collective-permute-done.15.refs_5_) | copy-start | bytes 1572868
  381.0 14.7 %copy-start.6 = (f32[256,512]{1,0:T(8,128)}, f32[256,512]{1,0:T(8,128)S(1)}, u32[]{:S(2)}) copy-start(f32[256,512]{1,0:T(8,128)S(1)} %collective-permute-done.16.refs_6_) | copy-start | bytes 1572868
